TPU v7x, 256 devices: a whole 4x4x8 slice. The times are simulated.
256 devices in a mesh: dp: 32 (over z_lo, x, y), tensor: 8 (over z_hi, core).
Axes of the slice: x: 4, y: 4, z: 8 (z_hi: 4, z_lo: 2; z = z_hi * 2 + z_lo), core: 2. Of those that a mesh axis runs over, the one named last changes fastest.
Arguments:
- hidden: bfloat16 [16384, 4096], P(('dp', 'tensor')), may hold values from -24 to 24
- adapter: bfloat16 [4096, 9216], P(None, 'tensor'), may hold values from -0.09375 to 0.09375
- teacher_rows: bfloat16 [16384, 9216], P('dp', 'tensor')
- scale_exps: int32 [16384], P('dp'), may hold values from -1 to 1
- packing: int32 [16384], P('dp'), may hold values from 0 to 16383, as said below
Outputs:
- row_grad: bfloat16 [16384, 4096], P(('dp', 'tensor'))
- weight_grad: bfloat16 [4096, 9216], P('dp', 'tensor')
Inputs may be any that keep to these rules, and one draw needn't show every extreme that they name: packing is a permutation of the tokens; each aligned block of 512 packed rows holds exactly 16 tokens of each block of 512 consecutive tokens.
All inputs are finite; a program needn't handle non-finite values.
Results may differ from a plain program's by a relative error of at most 0.0036.
Values may be sent and summed in bfloat16 or wider, within the bound.
No kernel may reach another device: no remote copies, remote signals or barrier semaphores. Data moves between devices by JAX's collectives and lax.ppermute only.
A program may use at most 128 MiB of HBM per device.

v0:
```python
import jax
import jax.numpy as jnp
from jax import lax
from jax.sharding import PartitionSpec as P

TW = 9216


def on_device(hidden, adapter, teacher_rows, scale_exps, packing):
    tok_dev = teacher_rows.shape[0]
    width_local = teacher_rows.shape[1]
    peers = lax.axis_size("dp")
    share = tok_dev // peers
    target_peer = packing // tok_dev
    sorter = jnp.argsort(target_peer)
    sent_rows = teacher_rows[sorter].reshape(peers, share, width_local)
    sent_exps = scale_exps[sorter].reshape(peers, share)
    sent_slots = (packing[sorter] % tok_dev).reshape(peers, share)
    got_rows, got_exps, got_slots = (
        lax.all_to_all(sent_rows, "dp", split_axis=0, concat_axis=0, tiled=True),
        lax.all_to_all(sent_exps, "dp", split_axis=0, concat_axis=0, tiled=True),
        lax.all_to_all(sent_slots, "dp", split_axis=0, concat_axis=0, tiled=True),
    )
    placing = jnp.argsort(got_slots.reshape(tok_dev))
    scales = jnp.exp2(got_exps.reshape(tok_dev)[placing].astype(jnp.float32))
    target = got_rows.reshape(tok_dev, width_local)[placing].astype(jnp.float32) * scales[:, None]
    whole = lax.all_gather(hidden, "tensor", axis=0, tiled=True)
    projected = jnp.dot(whole, adapter, preferred_element_type=jnp.float32)
    energy = lax.psum(jnp.sum(target * target, axis=1), "tensor") / TW + 1e-05
    delta = ((projected - target) / energy[:, None]).astype(jnp.bfloat16)
    row_total = lax.psum_scatter(
        lax.dot_general(
            delta, adapter, (((1,), (1,)), ((), ())), preferred_element_type=jnp.float32
        ),
        "tensor",
        scatter_dimension=0,
        tiled=True,
    )
    full_term = lax.dot_general(
        whole, delta, (((0,), (0,)), ((), ())), preferred_element_type=jnp.float32
    )
    weight_total = lax.psum_scatter(full_term, "dp", scatter_dimension=0, tiled=True)
    return (row_total.astype(jnp.bfloat16), (weight_total / tok_dev).astype(jnp.bfloat16))


def solution(mesh):
    placed = (P(("dp", "tensor"), None), P(None, "tensor"), P("dp", "tensor"), P("dp"), P("dp"))
    return jax.shard_map(
        on_device,
        mesh=mesh,
        in_specs=placed,
        out_specs=(P(("dp", "tensor"), None), P("dp", "tensor")),
        check_vma=False,
    )
```

profile of v0, /device:TPU:6, one launch (start us, length us, event | category | flops | bytes accessed | tf_op | source)
XLA Modules:
  0.0 436.9 jit_solution(15077355515006999561)
XLA Ops:
  7.2 0.7 all-gather.2.cloned.1.call-update
  7.9 0.7 add_select_fusion.1
  8.6 3.8 sort.31
  12.4 3.6 gather_fusion.1
  16.1 0.6 add_select_fusion
  16.7 8.9 %all-to-all-start.1 = ((s32[32,1,16]{2,1,0:T(1,128)}), s32[32,1,16]{2,1,0:T(1,128)S(1)}, u32[]{:S(2)}, u32[]{:S(2)}) async-start(s32[32,1,16]{2,1,0:T(1,128)} %bitcast.2), calls=%async_computation.1 | async-start | bytes 32768 | tf_op jit(solution)/shard_map/all_to_all | solution.py:22
  25.7 3.5 gather_fusion.3
  29.2 0.7 all_to_all.15
  29.9 2.2 all-to-all-done.1
  32.0 6.2 %all-to-all-start.2 = ((s32[32,1,16]{2,1,0:T(1,128)}), s32[32,1,16]{2,1,0:T(1,128)S(1)}, u32[]{:S(2)}, u32[]{:S(2)}) async-start(s32[32,1,16]{2,1,0:T(1,128)} %bitcast.3), calls=%async_computation.2 | async-start | bytes 32768 | tf_op jit(solution)/shard_map/all_to_all | solution.py:21
  38.2 2.8 gather_fusion
  41.0 3.5 all-to-all-done.2
  44.6 6.0 %all-to-all-start = ((bf16[32,16,1152]{2,1,0:T(8,128)(2,1)}), bf16[32,16,1152]{2,1,0:T(8,128)(2,1)S(1)}, u32[]{:S(2)}, u32[]{:S(2)}) async-start(bf16[32,16,1152]{2,1,0:T(8,128)(2,1)} %bitcast), calls=%async_computation | async-start | bytes 2359296 | tf_op jit(solution)/shard_map/all_to_all | solution.py:20
  50.6 0.5 broadcast.86
  51.1 0.7 reduce.6
  51.9 0.7 reduce.7
  52.7 3.8 sort.32
  56.5 3.5 gather_fusion.4
  60.0 17.5 %all-to-all-done = bf16[32,16,1152]{2,1,0:T(8,128)(2,1)S(1)} async-done(((bf16[32,16,1152]{2,1,0:T(8,128)(2,1)}), bf16[32,16,1152]{2,1,0:T(8,128)(2,1)S(1)}, u32[]{:S(2)}, u32[]{:S(2)}) %all-to-all-start) | async-done | bytes 1179680 | tf_op jit(solution)/shard_map/all_to_all | solution.py:20
  77.4 2.1 gather_fusion.2
  79.6 0.4 multiply_reduce_fusion
  80.0 16.1 %psum.7 = f32[512]{0:T(512)S(1)} all-reduce(f32[512]{0:T(512)S(1)} %multiply_reduce_fusion), channel_id=1, replica_groups=mesh['dp'=32,'tensor'=8] {'tensor'}, use_global_device_ids=true, to_apply=%region_3.4 | all-reduce | flops 512 | bytes 4096 | tf_op jit(solution)/shard_map/psum | solution.py:29
  96.1 10.2 %fusion.1 = bf16[512,1152]{1,0:T(8,128)(2,1)S(1)} fusion(bf16[512,4096]{1,0:T(8,128)(2,1)} %all-gather.2.cloned.1.call-done, bf16[4096,1152]{1,0:T(8,128)(2,1)} %param.6, bf16[512,1152]{1,0:T(8,128)(2,1)S(1)} %gather_fusion.2, f32[512]{0:T(512)S(1)} %multiply_add_fusion, f32[512]{0:T(512)S(1)} %multiply_exponential_fusion), kind=kOutput, calls=%fused_computation.8 | convolution fusion | flops 4834787328 | bytes 15994880 | tf_op jit(solution)/shard_map/dot_general | solution.py:28
  106.4 1.0 copy-done.2
  107.4 11.5 %fusion.5 = f32[512,4096]{1,0:T(8,128)} fusion(bf16[512,1152]{1,0:T(8,128)(2,1)S(1)} %fusion.1, bf16[4096,1152]{1,0:T(8,128)(2,1)} %param.6), kind=kOutput, calls=%fused_computation.29 | convolution fusion | flops 4831838208 | bytes 19005440 | tf_op jit(solution)/shard_map/dot_general | solution.py:32
  119.0 1.2 copy-done.3
  120.2 11.1 %convolution_bitcast_fusion = f32[4096,1152]{0,1:T(8,128)} fusion(bf16[512,1152]{1,0:T(8,128)(2,1)S(1)} %copy-done.3, bf16[512,4096]{1,0:T(8,128)(2,1)} %all-gather.2.cloned.1.call-done), kind=kOutput, calls=%fused_computation.5 | convolution fusion | flops 4831838208 | bytes 24248320 | tf_op jit(solution)/shard_map/dot_general | solution.py:39
  131.3 82.1 %reduce-scatter.3.cloned.1.call-done = f32[64,4096]{1,0:T(8,128)} async-done(((f32[512,4096]{1,0:T(8,128)}), f32[64,4096]{1,0:T(8,128)}) %reduce-scatter.3.cloned.1.call-update) | async-done | bytes 1048592 | tf_op jit(solution)/shard_map/reduce_scatter | solution.py:31
  213.4 2.1 convert_element_type.22
  215.5 212.9 %reduce-scatter.5.cloned.1.call-done = f32[128,1152]{0,1:T(8,128)} async-done(((f32[4096,1152]{0,1:T(8,128)}), f32[128,1152]{0,1:T(8,128)}) %reduce-scatter.5.cloned.1.call-update) | async-done | bytes 589840 | tf_op jit(solution)/shard_map/reduce_scatter | solution.py:42
  428.3 1.1 multiply_convert_fusion
  429.4 0.9 copy.11
  (23 shorter events, 0.5 us)
Async XLA Ops:
  7.2 31.0 %copy-start = (bf16[512,1152]{1,0:T(8,128)(2,1)S(1)}, bf16[512,1152]{1,0:T(8,128)(2,1)}, u32[]{:S(2)}) copy-start(bf16[512,1152]{1,0:T(8,128)(2,1)} %param.7) | copy-start | bytes 3538948
  7.2 18.5 %copy-start.1 = (s32[512]{0:T(512)S(1)}, s32[512]{0:T(512)}, u32[]{:S(2)}) copy-start(s32[512]{0:T(512)} %param.8) | copy-start | bytes 6148
  7.2 88.9 %all-gather.2.cloned.1.call-start = ((), (), s32[]{:S(2)}) async-start(), calls=%async_computation.5 | async-start | bytes 4718592 | tf_op jit(solution)/shard_map/all_gather | solution.py:27
  16.7 15.3 %all-to-all-start.1 = ((s32[32,1,16]{2,1,0:T(1,128)}), s32[32,1,16]{2,1,0:T(1,128)S(1)}, u32[]{:S(2)}, u32[]{:S(2)}) async-start(s32[32,1,16]{2,1,0:T(1,128)} %bitcast.2), calls=%async_computation.1 | async-start | bytes 32768 | tf_op jit(solution)/shard_map/all_to_all | solution.py:22
  32.0 12.6 %all-to-all-start.2 = ((s32[32,1,16]{2,1,0:T(1,128)}), s32[32,1,16]{2,1,0:T(1,128)S(1)}, u32[]{:S(2)}, u32[]{:S(2)}) async-start(s32[32,1,16]{2,1,0:T(1,128)} %bitcast.3), calls=%async_computation.2 | async-start | bytes 32768 | tf_op jit(solution)/shard_map/all_to_all | solution.py:21
  44.6 32.9 %all-to-all-start = ((bf16[32,16,1152]{2,1,0:T(8,128)(2,1)}), bf16[32,16,1152]{2,1,0:T(8,128)(2,1)S(1)}, u32[]{:S(2)}, u32[]{:S(2)}) async-start(bf16[32,16,1152]{2,1,0:T(8,128)(2,1)} %bitcast), calls=%async_computation | async-start | bytes 2359296 | tf_op jit(solution)/shard_map/all_to_all | solution.py:20
  50.5 162.9 %reduce-scatter.3.cloned.1.call-start = ((), (), s32[]{:S(2)}) async-start(), calls=%async_computation.6 | async-start | bytes 9437184 | tf_op jit(solution)/shard_map/reduce_scatter | solution.py:31
  106.3 1.0 copy-start.2
  118.9 1.3 copy-start.3
  118.9 309.4 %reduce-scatter.5.cloned.1.call-start = ((), (), s32[]{:S(2)}) async-start(), calls=%async_computation.7 | async-start | bytes 19464192 | tf_op jit(solution)/shard_map/reduce_scatter | solution.py:42
Sparse Core Ops, SparseCore 0:
  9.9 61.5 all-gather.1
  119.0 94.3 reduce-scatter.2
  216.0 212.3 reduce-scatter.4
where the time goes:
time: 444 us; the launch traced here: 437 us
  waiting for transfers between devices  319 us (72%)
  matrix products  32.9 us (7%)
  starting transfers between devices  21.2 us (5%)
  local copies, waits for them, and re-layouts  20.1 us (5%)
  blocking collectives  16.1 us (4%)
  other arithmetic  13.9 us (3%)
  between operations  13.9 us (3%)
    reduce_scatter x1, waiting for transfers between devices, on_device(): lax.psum_scatter(full_term, 'dp', scatter_dimension=0, tiled=True)  213 us
    reduce_scatter x1, waiting for transfers between devices, on_device(): lax.psum_scatter(lax.dot_general(delta, adapter, (((1,), (1,)), ((), ()))...  82.1 us
    all_to_all x1, waiting for transfers between devices, on_device(): lax.all_to_all(sent_rows, 'dp', split_axis=0, concat_axis=0, tiled=True)  17.5 us
    psum x1, blocking collectives, on_device(): energy = lax.psum(jnp.sum(target * target, axis=1), 'tensor') / TW + 1e-05  16.1 us
    dot_general x1, matrix products, on_device(): lax.dot_general(delta, adapter, (((1,), (1,)), ((), ())), preferred_eleme...  11.5 us
    dot_general x1, matrix products, on_device(): lax.dot_general(whole, delta, (((0,), (0,)), ((), ())), preferred_element...  11.1 us
    dot_general x1, matrix products, on_device(): projected = jnp.dot(whole, adapter, preferred_element_type=jnp.float32)  10.2 us
    all_to_all x1, starting transfers between devices, on_device(): lax.all_to_all(sent_slots, 'dp', split_axis=0, concat_axis=0, tiled=True)  8.92 us
  transfers between devices with their start and end apart: 6, of which 5 were waited for; matrix products, arithmetic and copies ran while one was open for 9% of the time, Pallas kernels for 0%

commit v1 on v0

v1 whole, which is shorter than its diff:
```python
import functools

import jax
import jax.numpy as jnp
from jax import lax
from jax.experimental import pallas as pl
from jax.experimental.pallas import tpu as pltpu
from jax.sharding import PartitionSpec as P

TW = 9216
META = 128
F32, BF16 = jnp.float32, jnp.bfloat16


def params(mib):
    return pltpu.CompilerParams(vmem_limit_bytes=mib << 20)


LIGHT = pl.CostEstimate(flops=0, bytes_accessed=0, transcendentals=0)


def iota(shape, axis):
    return lax.broadcasted_iota(jnp.int32, shape, axis)


def column(row):
    return jnp.broadcast_to(row.astype(F32), (META, row.shape[1])).T


def as_row(col):
    return jnp.broadcast_to(col, (col.shape[0], META)).T[:1]


def scale_of(exps):
    return jnp.where(exps > 0.5, 2.0, jnp.where(exps < -0.5, 0.5, 1.0))


def squares_kernel(exps_ref, rows_ref, squares_ref):
    rows = rows_ref[...].astype(F32)
    scale = scale_of(exps_ref[...].astype(F32))
    squares_ref[...] = as_row(jnp.sum(rows * rows, axis=1, keepdims=True)) * (scale * scale)


def sum_kernel(*refs):
    total = refs[0][...]
    for ref in refs[1:-1]:
        total = total + ref[...]
    refs[-1][...] = total


def pack_kernel(share, where_ref, packing_ref, exps_ref, s0_ref, s1_ref, s2_ref, s3_ref, rows_ref, keep_ref, leave_ref):
    tok, width = rows_ref.shape
    packing = packing_ref[...]
    peer = packing // tok
    slot = packing % tok
    plane = tok // share // 2
    peer = jnp.where(peer // plane == where_ref[0], 0, plane) + peer % plane
    earlier = iota((tok, tok), 0) < iota((tok, tok), 1)
    same = (column(peer)[:, :1] == peer.astype(F32)) & earlier
    rank = jnp.sum(jnp.where(same, 1.0, 0.0), axis=0, keepdims=True)
    place = peer * share + rank.astype(jnp.int32)
    pick = jnp.where(iota((tok, tok), 0) == place, 1.0, 0.0).astype(BF16)
    lane = iota((tok, META), 1)
    meta = jnp.where(lane == 0, column(slot // 16), 0.0)
    meta = jnp.where(lane == 1, column(slot % 16), meta)
    meta = jnp.where(lane == 2, column(exps_ref[...]), meta)
    rest = column(s0_ref[...] + s1_ref[...] + s2_ref[...] + s3_ref[...])
    for k in range(3):
        term = rest.astype(BF16).astype(F32)
        meta = jnp.where(lane == 3 + k, term, meta)
        rest = rest - term
    rows = jnp.dot(pick, rows_ref[...], preferred_element_type=F32).astype(BF16)
    meta = jnp.dot(pick, meta.astype(BF16), preferred_element_type=F32).astype(BF16)
    half = tok // 2
    for out_ref, at in ((keep_ref, 0), (leave_ref, half)):
        out_ref[:, :width] = rows[at : at + half]
        out_ref[:, width:] = meta[at : at + half]


def merge_kernel(share, keep_ref, came_ref, out_ref):
    for side, rows_ref in enumerate((keep_ref, came_ref)):
        for peer in range(rows_ref.shape[0] // share):
            out_ref[peer, side * share : (side + 1) * share, :] = rows_ref[peer * share : (peer + 1) * share, :]


def place_kernel(got_ref, target_ref, energy_ref):
    tok, width = target_ref.shape
    meta = got_ref[:, width:].astype(F32).T
    slot = (meta[0:1] * 16.0 + meta[1:2]).astype(jnp.int32)
    here = iota((tok, tok), 0) == slot
    pick = jnp.where(here, 1.0, 0.0).astype(BF16)

    def placed(row):
        return jnp.sum(jnp.where(here, row, 0.0), axis=1, keepdims=True)

    rows = jnp.dot(pick, got_ref[:, :width], preferred_element_type=F32)
    target_ref[...] = (rows * placed(scale_of(meta[2:3]))).astype(BF16)
    squares = placed(meta[3:4] + meta[4:5] + meta[5:6])
    energy_ref[...] = jnp.broadcast_to(squares / TW + 1e-05, (tok, META))


def project_kernel(own_ref, sib_ref, adapter_ref, out_ref):
    rows = jnp.concatenate([own_ref[...], sib_ref[...]], axis=0)
    out_ref[...] = jnp.dot(rows, adapter_ref[...], preferred_element_type=F32)


def project_call(own, sib, adapter):
    half, depth = own.shape
    width = adapter.shape[1]
    tile = 384
    return pl.pallas_call(
        project_kernel,
        out_shape=jax.ShapeDtypeStruct((2 * half, width), F32),
        grid=(width // tile,),
        in_specs=[
            pl.BlockSpec((half, depth), lambda n: (0, 0)),
            pl.BlockSpec((half, depth), lambda n: (0, 0)),
            pl.BlockSpec((depth, tile), lambda n: (0, n)),
        ],
        out_specs=pl.BlockSpec((2 * half, tile), lambda n: (0, n)),
        compiler_params=params(14),
        cost_estimate=LIGHT,
        name="project",
    )(own, sib, adapter)


def delta_kernel(where_ref, p0_ref, p1_ref, p2_ref, p3_ref, target_ref, energy_ref, delta_ref):
    half = p0_ref.shape[0] // 2
    zh, core = where_ref[3], where_ref[4]
    step = 1 - 2 * core
    for s, p_ref in enumerate((p0_ref, p1_ref, p2_ref, p3_ref)):
        mine = ((zh - step * s + 4) % 4) * 2 + core
        sibs = ((zh + step * s + 4) % 4) * 2 + 1 - core
        for side, block in enumerate((mine, sibs)):
            token = pl.ds(pl.multiple_of(block * half, half), half)
            diff = p_ref[side * half : (side + 1) * half, :] - target_ref[token, :].astype(F32)
            at = (2 * s + side) * half
            delta_ref[at : at + half, :] = (diff / energy_ref[token, :1]).astype(BF16)


def row_kernel(delta_ref, adapter_ref, *refs):
    keeps, send_ref = refs[:4], refs[4]
    half = keeps[0].shape[0]
    term = lax.dot_general(delta_ref[...], adapter_ref[...], (((1,), (1,)), ((), ())), preferred_element_type=F32)
    for s in range(4):
        keeps[s][...] = term[2 * s * half : (2 * s + 1) * half]
        send_ref[s * half : (s + 1) * half, :] = term[(2 * s + 1) * half : (2 * s + 2) * half].astype(BF16)


def row_call(delta, adapter):
    tok, width = delta.shape
    half = tok // 8
    depth = adapter.shape[0]
    tile = 512
    return pl.pallas_call(
        row_kernel,
        out_shape=(jax.ShapeDtypeStruct((half, depth), F32),) * 4 + (jax.ShapeDtypeStruct((4 * half, depth), BF16),),
        grid=(depth // tile,),
        in_specs=[
            pl.BlockSpec((tok, width), lambda n: (0, 0)),
            pl.BlockSpec((tile, width), lambda n: (n, 0)),
        ],
        out_specs=(pl.BlockSpec((half, tile), lambda n: (0, n)),) * 4
        + (pl.BlockSpec((4 * half, tile), lambda n: (0, n)),),
        compiler_params=params(11),
        cost_estimate=LIGHT,
        name="row_terms",
    )(delta, adapter)


def weight_kernel(k, with_came, turn, where_ref, *refs):
    hidden, delta = refs[:8], refs[8]
    came = refs[9:11] if with_came else (None, None)
    outs, left = refs[9 + 2 * with_came : -1], refs[-1]
    half = hidden[0].shape[0]
    x, y, core = where_ref[1], where_ref[2], where_ref[4]
    ahead = k * (1 - 2 * core) + 4
    for chunk in range(2):
        for j in range(4):
            if chunk == 0:
                block = ((x + ahead) % 4) * 4 + (y + j) % 4
            else:
                block = 16 + ((x + j) % 4) * 4 + (y + ahead) % 4
            columns = pl.ds(pl.multiple_of(block * 128, 128), 128)
            for part in range(8):
                left[part * half : (part + 1) * half, j * 128 : (j + 1) * 128] = hidden[part][:, columns]
        term = lax.dot_general(left[...], delta[...], (((0,), (0,)), ((), ())), preferred_element_type=F32)
        if with_came:
            term = term + came[chunk][...].astype(F32)
        if turn:
            for j in range(4):
                out = outs[4 * chunk + j]
                out[...] = term[128 * j : 128 * (j + 1)].astype(out.dtype)
        else:
            outs[chunk][...] = term.astype(BF16)


def weight_call(k, where, hidden, delta, came=()):
    tokens = 8 * hidden[0].shape[0]
    width = delta.shape[1]
    vmem = pl.BlockSpec(memory_space=pltpu.VMEM)
    turn = k == 0
    if turn:
        kinds = [jax.ShapeDtypeStruct((128, width), F32)] + [jax.ShapeDtypeStruct((128, width), BF16)] * 3
    else:
        kinds = [jax.ShapeDtypeStruct((512, width), BF16)]
    return pl.pallas_call(
        functools.partial(weight_kernel, k, len(came) > 0, turn),
        out_shape=tuple(kinds * 2),
        in_specs=[pl.BlockSpec(memory_space=pltpu.SMEM)] + [vmem] * (9 + len(came)),
        out_specs=(vmem,) * (2 * len(kinds)),
        scratch_shapes=[pltpu.VMEM((tokens, 512), BF16)],
        compiler_params=params(18),
        cost_estimate=LIGHT,
        name=f"weight_{k}",
    )(where, *hidden, delta, *came)


def light(kernel, name, out_shape, mib, *args, scalars=0):
    vmem = pl.BlockSpec(memory_space=pltpu.VMEM)
    return pl.pallas_call(
        kernel,
        out_shape=tuple(out_shape),
        in_specs=[pl.BlockSpec(memory_space=pltpu.SMEM)] * scalars + [vmem] * (len(args) - scalars),
        out_specs=(vmem,) * len(out_shape),
        compiler_params=params(mib),
        cost_estimate=LIGHT,
        name=name,
    )(*args)


def shard_kernel(where, own_a, a1, a2, a3, own_b, b1, b2, b3, stay, leave):
    sum_a = own_a[...] + a1[...].astype(F32) + a2[...].astype(F32) + a3[...].astype(F32)
    sum_b = own_b[...] + b1[...].astype(F32) + b2[...].astype(F32) + b3[...].astype(F32)
    low = where[0] == 0
    stay[...] = jnp.where(low, sum_a, sum_b)
    leave[...] = jnp.where(low, sum_b, sum_a).astype(BF16)


def weight_out_kernel(tokens, stay, came, out):
    out[...] = ((stay[...] + came[...].astype(F32)) / tokens).astype(BF16)


def row_out_kernel(pair, came, out):
    out[...] = (pair[...] + came[...].astype(F32)).astype(BF16)


def pair_kernel(k0, k1, k2, k3, swapped, *outs):
    half = k0.shape[0]
    for s, keep in enumerate((k0, k1, k2, k3)):
        total = keep[...] + swapped[s * half : (s + 1) * half, :].astype(F32)
        outs[s][...] = total.astype(outs[s].dtype)


def on_device(hidden, adapter, teacher_rows, scale_exps, packing):
    tok, width = teacher_rows.shape
    half = hidden.shape[0]
    peers = lax.axis_size("dp")
    dp, tensor = lax.axis_index("dp"), lax.axis_index("tensor")
    zl, x, y = dp // 16, (dp // 4) % 4, dp % 4
    zh, core = tensor // 2, tensor % 2

    def over_dp(move):
        pairs = []
        for i in range(32):
            a, b, c = move(i // 16, (i // 4) % 4, i % 4)
            pairs.append((i, (a % 2) * 16 + (b % 4) * 4 + c % 4))
        return lambda value: lax.ppermute(value, "dp", pairs)

    def over_tensor(move):
        pairs = []
        for i in range(8):
            a, b = move(i // 2, i % 2)
            pairs.append((i, (a % 4) * 2 + b % 2))
        return lambda value: lax.ppermute(value, "tensor", pairs)

    def by_core(move):
        pairs = []
        for i in range(256):
            d, t = i // 8, i % 8
            b, c = move((d // 4) % 4, d % 4, 1 - 2 * (t % 2))
            pairs.append((i, ((d // 16) * 16 + (b % 4) * 4 + c % 4) * 8 + t))
        return lambda value: lax.ppermute(value, ("dp", "tensor"), pairs)

    x_ring = by_core(lambda b, c, way: (b + way, c))
    y_ring = by_core(lambda b, c, way: (b, c + way))
    x_forth, x_back = over_dp(lambda a, b, c: (a, b + 1, c)), over_dp(lambda a, b, c: (a, b - 1, c))
    y_forth, y_back = over_dp(lambda a, b, c: (a, b, c + 1)), over_dp(lambda a, b, c: (a, b, c - 1))
    x_across, y_across = over_dp(lambda a, b, c: (a, b + 2, c)), over_dp(lambda a, b, c: (a, b, c + 2))
    z_swap = over_dp(lambda a, b, c: (a + 1, b, c))
    core_swap = over_tensor(lambda a, b: (a, b + 1))
    chain = over_tensor(lambda a, b: (a + 1 - 2 * b, b))

    where = jnp.stack([zl, x, y, zh, core]).astype(jnp.int32)
    row = jax.ShapeDtypeStruct((1, tok), F32)
    share = tok // peers
    lanes = width + META
    packing, scale_exps = packing.reshape(1, tok), scale_exps.reshape(1, tok)

    own = [hidden, chain(hidden)]
    squares = light(squares_kernel, "squares", (row,), 10, scale_exps, teacher_rows)[0]
    squares = light(sum_kernel, "pair_squares", (row,), 4, squares, core_swap(squares))[0]
    others = [over_tensor(lambda a, b, k=k: (a + k, b))(squares) for k in (1, 2, 3)]
    half_rows = jax.ShapeDtypeStruct((tok // 2, lanes), BF16)
    keep, leave = light(
        functools.partial(pack_kernel, share), "pack", (half_rows, half_rows), 18,
        where, packing, scale_exps, squares, *others, teacher_rows, scalars=1,
    )
    own[1], keep = lax.optimization_barrier((own[1], keep))
    came = z_swap(leave)
    own.append(chain(own[1]))
    sib = [core_swap(block) for block in own]
    projected = [project_call(own[s], sib[s], adapter) for s in range(2)]
    came, *projected = lax.optimization_barrier((came, *projected))
    own.append(chain(own[2]))
    sib.append(core_swap(own[3]))
    projected += [project_call(own[s], sib[s], adapter) for s in range(2, 4)]
    merged = light(
        functools.partial(merge_kernel, share), "merge",
        (jax.ShapeDtypeStruct((peers // 2, 2 * share, lanes), BF16),), 10, keep, came,
    )[0]
    groups = [list(range(peers // 2)), list(range(peers // 2, peers))]
    got = lax.all_to_all(merged, "dp", 0, 0, axis_index_groups=groups, tiled=True)
    got, *projected[2:] = lax.optimization_barrier((got, *projected[2:]))
    target, energy = light(
        place_kernel, "place",
        (jax.ShapeDtypeStruct((tok, width), BF16), jax.ShapeDtypeStruct((tok, META), F32)), 16,
        got.reshape(tok, lanes),
    )
    delta = light(
        delta_kernel, "delta", (jax.ShapeDtypeStruct((tok, width), BF16),), 12,
        where, *projected, target, energy, scalars=1,
    )[0]

    held = [part for pair in zip(own, sib) for part in pair]
    ring_a, ring_b = weight_call(3, where, held, delta)
    came = (x_ring(ring_a), y_ring(ring_b))
    later, _ = lax.optimization_barrier((delta, ring_a))
    *keeps, send = row_call(later, adapter)
    *came, send = lax.optimization_barrier((*came, send))
    swapped = core_swap(send)
    ring_a, ring_b = weight_call(2, where, held, delta, came)
    came = (x_ring(ring_a), y_ring(ring_b))
    block = jax.ShapeDtypeStruct((half, hidden.shape[1]), F32)
    block16 = jax.ShapeDtypeStruct(block.shape, BF16)
    swapped, _ = lax.optimization_barrier((swapped, ring_a))
    pair = light(pair_kernel, "pair", (block, block16, block, block), 14, *keeps, swapped)
    total = chain(pair[1])
    *came, total = lax.optimization_barrier((*came, total))
    ring_a, ring_b = weight_call(1, where, held, delta, came)
    came = (x_ring(ring_a), y_ring(ring_b))
    total, _ = lax.optimization_barrier((total, ring_a))
    total = chain(light(row_out_kernel, "row_2", (block16,), 8, pair[2], total)[0])
    *came, total = lax.optimization_barrier((*came, total))
    own_a, a1, a2, a3, own_b, b1, b2, b3 = weight_call(0, where, held, delta, came)
    total, _ = lax.optimization_barrier((total, a1))
    total = chain(light(row_out_kernel, "row_3", (block16,), 8, pair[3], total)[0])
    came = (y_forth(a1), y_across(a2), y_back(a3), x_forth(b1), x_across(b2), x_back(b3))
    *came, total = lax.optimization_barrier((*came, total))
    part = jax.ShapeDtypeStruct((128, width), F32)
    part16 = jax.ShapeDtypeStruct((128, width), BF16)
    stay, leave = light(
        shard_kernel, "shard", (part, part16), 10, where, own_a, *came[:3], own_b, *came[3:], scalars=1,
    )
    weight_grad = light(
        functools.partial(weight_out_kernel, tok), "weight_out", (part16,), 8, stay, z_swap(leave)
    )[0]
    row_grad = light(row_out_kernel, "row_0", (block16,), 8, pair[0], total)[0]
    return row_grad, weight_grad


def solution(mesh):
    placed = (P(("dp", "tensor"), None), P(None, "tensor"), P("dp", "tensor"), P("dp"), P("dp"))
    return jax.shard_map(
        on_device,
        mesh=mesh,
        in_specs=placed,
        out_specs=(P(("dp", "tensor"), None), P("dp", "tensor")),
        check_vma=False,
    )
```

time: 444 us -> 190 us (0.43); the launches traced: 437 us -> 190 us
  waiting for transfers between devices: 319 us -> 91.8 us
  Pallas kernels: 0 us -> 38.2 us
  matrix products: 32.9 us -> 0 us
  blocking collectives: 16.1 us -> 0 us
  starting transfers between devices: 21.2 us -> 36.9 us
  other arithmetic: 13.9 us -> 0 us
  between operations: 13.9 us -> 0.98 us
    reduce_scatter x2 -> x0, waiting for transfers between devices: 295 us -> none  [the longest x1 213 us: on_device(): lax.psum_scatter(full_term, 'dp', scatter_dimension=0, tiled=True)]
    ppermute x0 -> x29, waiting for transfers between devices: none -> 91.8 us  [the longest x15 37.2 us: over_tensor(): return lambda value: lax.ppermute(value, 'tensor', pairs)]
    pallas_call x0 -> x21, Pallas kernels: none -> 38.2 us  [the longest x4 12.6 us: project_call(): pl.pallas_call(project_kernel, out_shape=jax.ShapeDtypeStruct((2 * half,...]
    dot_general x3 -> x0, matrix products: 32.9 us -> none  [the longest x1 11.5 us: on_device(): lax.dot_general(delta, adapter, (((1,), (1,)), ((), ())), preferred_eleme...]
    ppermute x0 -> x29, starting transfers between devices: none -> 29.5 us  [the longest x15 15 us: over_tensor(): return lambda value: lax.ppermute(value, 'tensor', pairs)]
    all_to_all x3 -> x1, waiting for transfers between devices: 23.2 us -> 0.01 us  [on_device(): lax.all_to_all(merged, 'dp', 0, 0, axis_index_groups=groups, tiled=True)]
    unnamed x9 -> x46, local copies, waits for them, and re-layouts: 3.1 us -> 21.6 us
    psum x1 -> x0, blocking collectives: 16.1 us -> none  [on_device(): energy = lax.psum(jnp.sum(target * target, axis=1), 'tensor') / TW + 1e-05]
  transfers between devices with their start and end apart: 6 -> 30, of which waited for: 5 -> 16; matrix products, arithmetic and copies ran while one was open for 9% -> 0% of each run, Pallas kernels for 0% -> 14%
where the time goes in v1:
time: 190 us
  waiting for transfers between devices  91.8 us (48%)
  Pallas kernels  38.2 us (20%)
  starting transfers between devices  36.9 us (19%)
  local copies, waits for them, and re-layouts  21.6 us (11%)
    ppermute x15, waiting for transfers between devices, over_tensor(): return lambda value: lax.ppermute(value, 'tensor', pairs)  37.2 us
    ppermute x8, waiting for transfers between devices, over_dp(): return lambda value: lax.ppermute(value, 'dp', pairs)  33.5 us
    unnamed x46, local copies, waits for them, and re-layouts  21.6 us
    ppermute x6, waiting for transfers between devices, by_core(): return lambda value: lax.ppermute(value, ('dp', 'tensor'), pairs)  21.2 us
    ppermute x15, starting transfers between devices, over_tensor(): return lambda value: lax.ppermute(value, 'tensor', pairs)  15 us
    pallas_call x4, Pallas kernels, project_call(): pl.pallas_call(project_kernel, out_shape=jax.ShapeDtypeStruct((2 * half,...  12.6 us
    pallas_call x4, Pallas kernels, weight_call(): pl.pallas_call(functools.partial(weight_kernel, k, len(came) > 0, turn),...  9.42 us
    pallas_call x12, Pallas kernels, light(): pl.pallas_call(kernel, out_shape=tuple(out_shape), in_specs=[pl.BlockSpec...  8.67 us
  transfers between devices with their start and end apart: 30, of which 16 were waited for; matrix products, arithmetic and copies ran while one was open for 0% of the time, Pallas kernels for 14%

profile of v1, /device:TPU:6, one launch (start us, length us, event | category | flops | bytes accessed | tf_op | source)
XLA Modules:
  0.0 189.5 jit_solution(15370888941747459483)
XLA Ops:
  0.6 3.3 %collective-permute-start.6 = (bf16[64,4096]{1,0:T(8,128)(2,1)}, bf16[64,4096]{1,0:T(8,128)(2,1)S(1)}, u32[]{:S(2)}, u32[]{:S(2)}) collective-permute-start(bf16[64,4096]{1,0:T(8,128)(2,1)} %refs_0_.7), channel_id=1, source_target_pairs={{0,2},{1,7},{2,4},{3,1},{4,6},{5,3},{6,0},{7,5},{8,10},{9,15},{10,... | collective-permute-start | bytes 1572872 | tf_op jit(solution)/shard_map/ppermute | solution.py:275
  6.3 2.7 %collective-permute-start = (f32[1,512]{1,0:T(1,128)S(1)}, f32[1,512]{1,0:T(1,128)S(1)}, u32[]{:S(2)}, u32[]{:S(2)}) collective-permute-start(f32[1,512]{1,0:T(1,128)S(1)} %squares.1.refs_0_), channel_id=1, source_target_pairs={{0,1},{1,0},{2,3},{3,2},{4,5},{5,4},{6,7},{7,6},{8,9},{9,8},{10,11... | collective-permute-start | bytes 6152 | tf_op jit(solution)/shard_map/ppermute | solution.py:275
  11.2 4.4 %collective-permute-start.2 = (f32[1,512]{1,0:T(1,128)S(1)}, f32[1,512]{1,0:T(1,128)S(1)}, u32[]{:S(2)}, u32[]{:S(2)}) collective-permute-start(f32[1,512]{1,0:T(1,128)S(1)} %pair_squares.1.s0_ref), channel_id=1, source_target_pairs={{0,4},{1,5},{2,6},{3,7},{4,0},{5,1},{6,2},{7,3},{8,12},{9,13},{10,... | collective-permute-start | bytes 6152 | tf_op jit(solution)/shard_map/ppermute | solution.py:275
  15.9 6.6 %collective-permute-done.2.s2_ref = f32[1,512]{1,0:T(1,128)S(1)} collective-permute-done((f32[1,512]{1,0:T(1,128)S(1)}, f32[1,512]{1,0:T(1,128)S(1)}, u32[]{:S(2)}, u32[]{:S(2)}) %collective-permute-start.2) | collective-permute-done | bytes 2080 | tf_op jit(solution)/shard_map/ppermute | solution.py:275
  23.8 1.8 pack.1
  27.8 3.7 %copy-done = bf16[4096,1152]{1,0:T(8,128)(2,1)S(1)} copy-done((bf16[4096,1152]{1,0:T(8,128)(2,1)S(1)}, bf16[4096,1152]{1,0:T(8,128)(2,1)}, u32[]{:S(2)}) %copy-start) | copy-done | bytes 9437208
  31.4 3.2 %project.4.p0_ref = f32[128,1152]{1,0:T(8,128)S(1)} custom-call(bf16[64,4096]{1,0:T(8,128)(2,1)S(1)} %copy-done.4, bf16[64,4096]{1,0:T(8,128)(2,1)S(1)} %collective-permute-done.5.sib_ref.refs_1_, bf16[4096,1152]{1,0:T(8,128)(2,1)S(1)} %copy-done), custom_call_target="tpu_custom_call" | custom-call | tf_op jit(solution)/shard_map/project/pallas_call | solution.py:111
  35.1 3.2 %project.5.p1_ref = f32[128,1152]{1,0:T(8,128)S(1)} custom-call(bf16[64,4096]{1,0:T(8,128)(2,1)S(1)} %collective-permute-done.6.own_ref.refs_2_, bf16[64,4096]{1,0:T(8,128)(2,1)S(1)} %collective-permute-done.7.sib_ref.refs_3_, bf16[4096,1152]{1,0:T(8,128)(2,1)S(1)} %copy-done.1), custom_call_target="tpu_custom_call" | custom-call | tf_op jit(solution)/shard_map/project/pallas_call | solution.py:111
  39.1 9.9 %collective-permute-done.4.came_ref = bf16[256,1280]{1,0:T(8,128)(2,1)S(1)} collective-permute-done((bf16[256,1280]{1,0:T(8,128)(2,1)S(1)}, bf16[256,1280]{1,0:T(8,128)(2,1)S(1)}, u32[]{:S(2)}, u32[]{:S(2)}) %collective-permute-start.4) | collective-permute-done | bytes 655392 | tf_op jit(solution)/shard_map/ppermute | solution.py:268
  50.2 7.4 %all-to-all-start = ((bf16[16,32,1280]{2,1,0:T(8,128)(2,1)}), bf16[16,32,1280]{2,1,0:T(8,128)(2,1)}, u32[]{:S(2)}, u32[]{:S(2)}) async-start(bf16[16,32,1280]{2,1,0:T(8,128)(2,1)} %copy-done.9), calls=%async_computation | async-start | bytes 2621440 | tf_op jit(solution)/shard_map/all_to_all | solution.py:323
  57.8 15.6 %collective-permute-done.10.own_ref.refs_6_ = bf16[64,4096]{1,0:T(8,128)(2,1)S(1)} collective-permute-done((bf16[64,4096]{1,0:T(8,128)(2,1)S(1)}, bf16[64,4096]{1,0:T(8,128)(2,1)S(1)}, u32[]{:S(2)}, u32[]{:S(2)}) %collective-permute-start.10) | collective-permute-done | bytes 524320 | tf_op jit(solution)/shard_map/ppermute | solution.py:275
  73.5 3.7 %copy-done.2 = bf16[4096,1152]{1,0:T(8,128)(2,1)S(1)} copy-done((bf16[4096,1152]{1,0:T(8,128)(2,1)S(1)}, bf16[4096,1152]{1,0:T(8,128)(2,1)}, u32[]{:S(2)}) %copy-start.2) | copy-done | bytes 9437208
  77.1 3.2 %project.6.p2_ref = f32[128,1152]{1,0:T(8,128)S(1)} custom-call(bf16[64,4096]{1,0:T(8,128)(2,1)S(1)} %collective-permute-done.8.own_ref.refs_4_, bf16[64,4096]{1,0:T(8,128)(2,1)S(1)} %collective-permute-done.9.sib_ref.refs_5_, bf16[4096,1152]{1,0:T(8,128)(2,1)S(1)} %copy-done.2), custom_call_target="tpu_custom_call" | custom-call | tf_op jit(solution)/shard_map/project/pallas_call | solution.py:111
  81.1 3.2 %project.7.p3_ref = f32[128,1152]{1,0:T(8,128)S(1)} custom-call(bf16[64,4096]{1,0:T(8,128)(2,1)S(1)} %collective-permute-done.10.own_ref.refs_6_, bf16[64,4096]{1,0:T(8,128)(2,1)S(1)} %collective-permute-done.11.sib_ref.refs_7_, bf16[4096,1152]{1,0:T(8,128)(2,1)S(1)} %copy-done.2), custom_call_target="tpu_custom_call" | custom-call | tf_op jit(solution)/shard_map/project/pallas_call | solution.py:111
  86.0 2.5 %place.1 = (bf16[512,1152]{1,0:T(8,128)(2,1)S(1)}, f32[512,128]{1,0:T(8,128)S(1)}) custom-call(bf16[512,1280]{1,0:T(8,128)(2,1)} %bitcast.7.got_ref), custom_call_target="tpu_custom_call" | custom-call | tf_op jit(solution)/shard_map/place/pallas_call | solution.py:221
  91.8 2.3 %weight_3.1 = (bf16[512,1152]{1,0:T(8,128)(2,1)S(1)}, bf16[512,1152]{1,0:T(8,128)(2,1)S(1)}) custom-call(s32[5]{0:T(128)S(1)} %stack.23.where_ref.where, bf16[64,4096]{1,0:T(8,128)(2,1)S(1)} %copy-done.4, bf16[64,4096]{1,0:T(8,128)(2,1)S(1)} %collective-permute-done.5.sib_ref.refs_1_, bf16[64,4096]{1,0:T(8,128)(2,1)S(1)} %collective-permute-done.6.own_ref.refs_2_, ...), custom_call_target="tpu_custom_call" | custom-call | tf_op jit(solution)/shard_map/weight_3/pallas_call | solution.py:207
  96.3 3.7 %copy-done.3 = bf16[4096,1152]{1,0:T(8,128)(2,1)S(1)} copy-done((bf16[4096,1152]{1,0:T(8,128)(2,1)S(1)}, bf16[4096,1152]{1,0:T(8,128)(2,1)}, u32[]{:S(2)}) %copy-start.3) | copy-done | bytes 9437208
  99.9 7.5 %row_terms.1 = (f32[64,4096]{1,0:T(8,128)S(1)}, f32[64,4096]{1,0:T(8,128)S(1)}, f32[64,4096]{1,0:T(8,128)S(1)}, f32[64,4096]{1,0:T(8,128)S(1)}, bf16[256,4096]{1,0:T(8,128)(2,1)S(1)}) custom-call(bf16[512,1152]{1,0:T(8,128)(2,1)S(1)} %delta.1.refs_8_.delta_ref, bf16[4096,1152]{1,0:T(8,128)(2,1)S(1)} %copy-done.3), custom_call_target="tpu_custom_call" | custom-call | tf_op jit(solution)/shard_map/row_terms/pallas_call | solution.py:155
  107.4 4.3 %collective-permute-done.13.refs_10_ = bf16[512,1152]{1,0:T(8,128)(2,1)S(1)} collective-permute-done((bf16[512,1152]{1,0:T(8,128)(2,1)S(1)}, bf16[512,1152]{1,0:T(8,128)(2,1)S(1)}, u32[]{:S(2)}, u32[]{:S(2)}) %collective-permute-start.13) | collective-permute-done | bytes 1179680 | tf_op jit(solution)/shard_map/ppermute | solution.py:283
  113.4 2.4 %weight_2.1 = (bf16[512,1152]{1,0:T(8,128)(2,1)S(1)}, bf16[512,1152]{1,0:T(8,128)(2,1)S(1)}) custom-call(s32[5]{0:T(128)S(1)} %stack.23.where_ref.where, bf16[64,4096]{1,0:T(8,128)(2,1)S(1)} %copy-done.4, bf16[64,4096]{1,0:T(8,128)(2,1)S(1)} %collective-permute-done.5.sib_ref.refs_1_, bf16[64,4096]{1,0:T(8,128)(2,1)S(1)} %collective-permute-done.6.own_ref.refs_2_, ...), custom_call_target="tpu_custom_call" | custom-call | tf_op jit(solution)/shard_map/weight_2/pallas_call | solution.py:207
  118.2 15.0 %collective-permute-done.16.refs_10_ = bf16[512,1152]{1,0:T(8,128)(2,1)S(1)} collective-permute-done((bf16[512,1152]{1,0:T(8,128)(2,1)S(1)}, bf16[512,1152]{1,0:T(8,128)(2,1)S(1)}, u32[]{:S(2)}, u32[]{:S(2)}) %collective-permute-start.16) | collective-permute-done | bytes 1179680 | tf_op jit(solution)/shard_map/ppermute | solution.py:283
  133.3 2.4 %weight_1.1 = (bf16[512,1152]{1,0:T(8,128)(2,1)S(1)}, bf16[512,1152]{1,0:T(8,128)(2,1)S(1)}) custom-call(s32[5]{0:T(128)S(1)} %stack.23.where_ref.where, bf16[64,4096]{1,0:T(8,128)(2,1)S(1)} %copy-done.4, bf16[64,4096]{1,0:T(8,128)(2,1)S(1)} %collective-permute-done.5.sib_ref.refs_1_, bf16[64,4096]{1,0:T(8,128)(2,1)S(1)} %collective-permute-done.6.own_ref.refs_2_, ...), custom_call_target="tpu_custom_call" | custom-call | tf_op jit(solution)/shard_map/weight_1/pallas_call | solution.py:207
  135.7 2.9 %collective-permute-start.18 = (bf16[512,1152]{1,0:T(8,128)(2,1)S(1)}, bf16[512,1152]{1,0:T(8,128)(2,1)S(1)}, u32[]{:S(2)}, u32[]{:S(2)}) collective-permute-start(bf16[512,1152]{1,0:T(8,128)(2,1)S(1)} %get-tuple-element.89), channel_id=1, source_target_pairs={{0,32},{1,97},{2,34},{3,99},{4,36},{5,101},{6,38},{7,103},{8,40},{... | collective-permute-start | bytes 3538952 | tf_op jit(solution)/shard_map/ppermute | solution.py:283
  138.9 12.7 %collective-permute-done.20.came = bf16[64,4096]{1,0:T(8,128)(2,1)S(1)} collective-permute-done((bf16[64,4096]{1,0:T(8,128)(2,1)S(1)}, bf16[64,4096]{1,0:T(8,128)(2,1)S(1)}, u32[]{:S(2)}, u32[]{:S(2)}) %collective-permute-start.20) | collective-permute-done | bytes 524320 | tf_op jit(solution)/shard_map/ppermute | solution.py:275
  153.1 2.4 %weight_0.1 = (f32[128,1152]{1,0:T(8,128)S(1)}, bf16[128,1152]{1,0:T(8,128)(2,1)S(1)}, bf16[128,1152]{1,0:T(8,128)(2,1)S(1)}, bf16[128,1152]{1,0:T(8,128)(2,1)S(...) custom-call(s32[5]{0:T(128)S(1)} %stack.23.where_ref.where, ...), custom_call_target="tpu_custom_call" | custom-call | tf_op jit(solution)/shard_map/weight_0/pallas_call | solution.py:207
  155.5 2.4 %collective-permute-start.22 = (bf16[128,1152]{1,0:T(8,128)(2,1)S(1)}, bf16[128,1152]{1,0:T(8,128)(2,1)S(1)}, u32[]{:S(2)}, u32[]{:S(2)}) collective-permute-start(bf16[128,1152]{1,0:T(8,128)(2,1)S(1)} %get-tuple-element.97), channel_id=1, source_target_pairs={{0,16},{8,24},{16,0},{24,8},{32,48},{40,56},{48,32},{56,40},{64,80... | collective-permute-start | bytes 884744 | tf_op jit(solution)/shard_map/ppermute | solution.py:268
  158.5 3.1 %collective-permute-start.24 = (bf16[128,1152]{1,0:T(8,128)(2,1)S(1)}, bf16[128,1152]{1,0:T(8,128)(2,1)S(1)}, u32[]{:S(2)}, u32[]{:S(2)}) collective-permute-start(bf16[128,1152]{1,0:T(8,128)(2,1)S(1)} %get-tuple-element.99), channel_id=1, source_target_pairs={{0,32},{8,40},{16,48},{24,56},{32,64},{40,72},{48,80},{56,88},{64,... | collective-permute-start | bytes 884744 | tf_op jit(solution)/shard_map/ppermute | solution.py:268
  161.6 4.1 %collective-permute-done.22.a2 = bf16[128,1152]{1,0:T(8,128)(2,1)S(1)} collective-permute-done((bf16[128,1152]{1,0:T(8,128)(2,1)S(1)}, bf16[128,1152]{1,0:T(8,128)(2,1)S(1)}, u32[]{:S(2)}, u32[]{:S(2)}) %collective-permute-start.22) | collective-permute-done | bytes 294944 | tf_op jit(solution)/shard_map/ppermute | solution.py:268
  165.7 4.5 %collective-permute-done.23.a3 = bf16[128,1152]{1,0:T(8,128)(2,1)S(1)} collective-permute-done((bf16[128,1152]{1,0:T(8,128)(2,1)S(1)}, bf16[128,1152]{1,0:T(8,128)(2,1)S(1)}, u32[]{:S(2)}, u32[]{:S(2)}) %collective-permute-start.23) | collective-permute-done | bytes 294944 | tf_op jit(solution)/shard_map/ppermute | solution.py:268
  173.0 3.9 %collective-permute-done.26.b3 = bf16[128,1152]{1,0:T(8,128)(2,1)S(1)} collective-permute-done((bf16[128,1152]{1,0:T(8,128)(2,1)S(1)}, bf16[128,1152]{1,0:T(8,128)(2,1)S(1)}, u32[]{:S(2)}, u32[]{:S(2)}) %collective-permute-start.26) | collective-permute-done | bytes 294944 | tf_op jit(solution)/shard_map/ppermute | solution.py:268
  177.0 3.1 %collective-permute-done.21.a1 = bf16[128,1152]{1,0:T(8,128)(2,1)S(1)} collective-permute-done((bf16[128,1152]{1,0:T(8,128)(2,1)S(1)}, bf16[128,1152]{1,0:T(8,128)(2,1)S(1)}, u32[]{:S(2)}, u32[]{:S(2)}) %collective-permute-start.21) | collective-permute-done | bytes 294944 | tf_op jit(solution)/shard_map/ppermute | solution.py:268
  181.9 6.8 %collective-permute-done.28.came = bf16[128,1152]{1,0:T(8,128)(2,1)S(1)} collective-permute-done((bf16[128,1152]{1,0:T(8,128)(2,1)S(1)}, bf16[128,1152]{1,0:T(8,128)(2,1)S(1)}, u32[]{:S(2)}, u32[]{:S(2)}) %collective-permute-start.28) | collective-permute-done | bytes 294944 | tf_op jit(solution)/shard_map/ppermute | solution.py:268
  (96 shorter events, 30.9 us)
Async XLA Ops:
  0.6 25.2 %collective-permute-start.6 = (bf16[64,4096]{1,0:T(8,128)(2,1)}, bf16[64,4096]{1,0:T(8,128)(2,1)S(1)}, u32[]{:S(2)}, u32[]{:S(2)}) collective-permute-start(bf16[64,4096]{1,0:T(8,128)(2,1)} %refs_0_.7), channel_id=1, source_target_pairs={{0,2},{1,7},{2,4},{3,1},{4,6},{5,3},{6,0},{7,5},{8,10},{9,15},{10,... | collective-permute-start | bytes 1572872 | tf_op jit(solution)/shard_map/ppermute | solution.py:275
  5.9 16.6 %copy-start.22 = (s32[512]{0:T(512)S(1)}, s32[512]{0:T(512)}, u32[]{:S(2)}) copy-start(s32[512]{0:T(512)} %param.9) | copy-start | bytes 6148
  5.9 19.8 %copy-start.4 = (bf16[64,4096]{1,0:T(8,128)(2,1)S(1)}, bf16[64,4096]{1,0:T(8,128)(2,1)}, u32[]{:S(2)}) copy-start(bf16[64,4096]{1,0:T(8,128)(2,1)} %refs_0_.7) | copy-start | bytes 1572868
  6.3 3.5 %collective-permute-start = (f32[1,512]{1,0:T(1,128)S(1)}, f32[1,512]{1,0:T(1,128)S(1)}, u32[]{:S(2)}, u32[]{:S(2)}) collective-permute-start(f32[1,512]{1,0:T(1,128)S(1)} %squares.1.refs_0_), channel_id=1, source_target_pairs={{0,1},{1,0},{2,3},{3,2},{4,5},{5,4},{6,7},{7,6},{8,9},{9,8},{10,11... | collective-permute-start | bytes 6152 | tf_op jit(solution)/shard_map/ppermute | solution.py:275
  9.7 6.2 %collective-permute-start.3 = (f32[1,512]{1,0:T(1,128)S(1)}, f32[1,512]{1,0:T(1,128)S(1)}, u32[]{:S(2)}, u32[]{:S(2)}) collective-permute-start(f32[1,512]{1,0:T(1,128)S(1)} %pair_squares.1.s0_ref), channel_id=1, source_target_pairs={{0,6},{1,7},{2,0},{3,1},{4,2},{5,3},{6,4},{7,5},{8,14},{9,15},{10,... | collective-permute-start | bytes 6152 | tf_op jit(solution)/shard_map/ppermute | solution.py:275
  11.2 11.3 %collective-permute-start.2 = (f32[1,512]{1,0:T(1,128)S(1)}, f32[1,512]{1,0:T(1,128)S(1)}, u32[]{:S(2)}, u32[]{:S(2)}) collective-permute-start(f32[1,512]{1,0:T(1,128)S(1)} %pair_squares.1.s0_ref), channel_id=1, source_target_pairs={{0,4},{1,5},{2,6},{3,7},{4,0},{5,1},{6,2},{7,3},{8,12},{9,13},{10,... | collective-permute-start | bytes 6152 | tf_op jit(solution)/shard_map/ppermute | solution.py:275
  15.6 7.0 %collective-permute-start.1 = (f32[1,512]{1,0:T(1,128)S(1)}, f32[1,512]{1,0:T(1,128)S(1)}, u32[]{:S(2)}, u32[]{:S(2)}) collective-permute-start(f32[1,512]{1,0:T(1,128)S(1)} %pair_squares.1.s0_ref), channel_id=1, source_target_pairs={{0,2},{1,3},{2,4},{3,5},{4,6},{5,7},{6,0},{7,1},{8,10},{9,11},{10,... | collective-permute-start | bytes 6152 | tf_op jit(solution)/shard_map/ppermute | solution.py:275
  25.6 23.4 %collective-permute-start.4 = (bf16[256,1280]{1,0:T(8,128)(2,1)S(1)}, bf16[256,1280]{1,0:T(8,128)(2,1)S(1)}, u32[]{:S(2)}, u32[]{:S(2)}) collective-permute-start(bf16[256,1280]{1,0:T(8,128)(2,1)S(1)} %get-tuple-element.59), channel_id=1, source_target_pairs={{0,128},{8,136},{16,144},{24,152},{32,160},{40,168},{48,176},{56,1... | collective-permute-start | bytes 1966088 | tf_op jit(solution)/shard_map/ppermute | solution.py:268
  25.8 2.0 %collective-permute-start.5 = (bf16[64,4096]{1,0:T(8,128)(2,1)S(1)}, bf16[64,4096]{1,0:T(8,128)(2,1)S(1)}, u32[]{:S(2)}, u32[]{:S(2)}) collective-permute-start(bf16[64,4096]{1,0:T(8,128)(2,1)S(1)} %copy-done.4), channel_id=1, source_target_pairs={{0,1},{1,0},{2,3},{3,2},{4,5},{5,4},{6,7},{7,6},{8,9},{9,8},{10,11... | collective-permute-start | bytes 1572872 | tf_op jit(solution)/shard_map/ppermute | solution.py:275
  25.9 8.8 %collective-permute-start.7 = (bf16[64,4096]{1,0:T(8,128)(2,1)S(1)}, bf16[64,4096]{1,0:T(8,128)(2,1)S(1)}, u32[]{:S(2)}, u32[]{:S(2)}) collective-permute-start(bf16[64,4096]{1,0:T(8,128)(2,1)S(1)} %collective-permute-done.6.own_ref.refs_2_), channel_id=1, source_target_pairs={{0,1},{1,0},{2,3},{3,2},{4,5},{5,4},{6,7},{7,6},{8,9},{9,8},{10,11... | collective-permute-start | bytes 1572872 | tf_op jit(solution)/shard_map/ppermute | solution.py:275
  26.4 31.3 %collective-permute-start.8 = (bf16[64,4096]{1,0:T(8,128)(2,1)S(1)}, bf16[64,4096]{1,0:T(8,128)(2,1)S(1)}, u32[]{:S(2)}, u32[]{:S(2)}) collective-permute-start(bf16[64,4096]{1,0:T(8,128)(2,1)S(1)} %collective-permute-done.6.own_ref.refs_2_), channel_id=1, source_target_pairs={{0,2},{1,7},{2,4},{3,1},{4,6},{5,3},{6,0},{7,5},{8,10},{9,15},{10,... | collective-permute-start | bytes 1572872 | tf_op jit(solution)/shard_map/ppermute | solution.py:275
  50.2 35.8 %all-to-all-start = ((bf16[16,32,1280]{2,1,0:T(8,128)(2,1)}), bf16[16,32,1280]{2,1,0:T(8,128)(2,1)}, u32[]{:S(2)}, u32[]{:S(2)}) async-start(bf16[16,32,1280]{2,1,0:T(8,128)(2,1)} %copy-done.9), calls=%async_computation | async-start | bytes 2621440 | tf_op jit(solution)/shard_map/all_to_all | solution.py:323
  57.6 15.8 %collective-permute-start.10 = (bf16[64,4096]{1,0:T(8,128)(2,1)S(1)}, bf16[64,4096]{1,0:T(8,128)(2,1)S(1)}, u32[]{:S(2)}, u32[]{:S(2)}) collective-permute-start(bf16[64,4096]{1,0:T(8,128)(2,1)S(1)} %collective-permute-done.8.own_ref.refs_4_), channel_id=1, source_target_pairs={{0,2},{1,7},{2,4},{3,1},{4,6},{5,3},{6,0},{7,5},{8,10},{9,15},{10,... | collective-permute-start | bytes 1572872 | tf_op jit(solution)/shard_map/ppermute | solution.py:275
  57.7 15.8 %collective-permute-start.9 = (bf16[64,4096]{1,0:T(8,128)(2,1)S(1)}, bf16[64,4096]{1,0:T(8,128)(2,1)S(1)}, u32[]{:S(2)}, u32[]{:S(2)}) collective-permute-start(bf16[64,4096]{1,0:T(8,128)(2,1)S(1)} %collective-permute-done.8.own_ref.refs_4_), channel_id=1, source_target_pairs={{0,1},{1,0},{2,3},{3,2},{4,5},{5,4},{6,7},{7,6},{8,9},{9,8},{10,11... | collective-permute-start | bytes 1572872 | tf_op jit(solution)/shard_map/ppermute | solution.py:275
  73.5 7.7 %collective-permute-start.11 = (bf16[64,4096]{1,0:T(8,128)(2,1)S(1)}, bf16[64,4096]{1,0:T(8,128)(2,1)S(1)}, u32[]{:S(2)}, u32[]{:S(2)}) collective-permute-start(bf16[64,4096]{1,0:T(8,128)(2,1)S(1)} %collective-permute-done.10.own_ref.refs_6_), channel_id=1, source_target_pairs={{0,1},{1,0},{2,3},{3,2},{4,5},{5,4},{6,7},{7,6},{8,9},{9,8},{10,11... | collective-permute-start | bytes 1572872 | tf_op jit(solution)/shard_map/ppermute | solution.py:275
  94.2 17.5 %collective-permute-start.13 = (bf16[512,1152]{1,0:T(8,128)(2,1)S(1)}, bf16[512,1152]{1,0:T(8,128)(2,1)S(1)}, u32[]{:S(2)}, u32[]{:S(2)}) collective-permute-start(bf16[512,1152]{1,0:T(8,128)(2,1)S(1)} %get-tuple-element.77), channel_id=1, source_target_pairs={{0,8},{1,25},{2,10},{3,27},{4,12},{5,29},{6,14},{7,31},{8,16},{9,1... | collective-permute-start | bytes 3538952 | tf_op jit(solution)/shard_map/ppermute | solution.py:283
  95.7 16.2 %collective-permute-start.12 = (bf16[512,1152]{1,0:T(8,128)(2,1)S(1)}, bf16[512,1152]{1,0:T(8,128)(2,1)S(1)}, u32[]{:S(2)}, u32[]{:S(2)}) collective-permute-start(bf16[512,1152]{1,0:T(8,128)(2,1)S(1)} %get-tuple-element.71), channel_id=1, source_target_pairs={{0,32},{1,97},{2,34},{3,99},{4,36},{5,101},{6,38},{7,103},{8,40},{... | collective-permute-start | bytes 3538952 | tf_op jit(solution)/shard_map/ppermute | solution.py:283
  111.9 5.7 %collective-permute-start.14 = (bf16[256,4096]{1,0:T(8,128)(2,1)S(1)}, bf16[256,4096]{1,0:T(8,128)(2,1)S(1)}, u32[]{:S(2)}, u32[]{:S(2)}) collective-permute-start(bf16[256,4096]{1,0:T(8,128)(2,1)S(1)} %get-tuple-element.79), channel_id=1, source_target_pairs={{0,1},{1,0},{2,3},{3,2},{4,5},{5,4},{6,7},{7,6},{8,9},{9,8},{10,11... | collective-permute-start | bytes 6291464 | tf_op jit(solution)/shard_map/ppermute | solution.py:275
  115.8 17.5 %collective-permute-start.16 = (bf16[512,1152]{1,0:T(8,128)(2,1)S(1)}, bf16[512,1152]{1,0:T(8,128)(2,1)S(1)}, u32[]{:S(2)}, u32[]{:S(2)}) collective-permute-start(bf16[512,1152]{1,0:T(8,128)(2,1)S(1)} %get-tuple-element.85), channel_id=1, source_target_pairs={{0,8},{1,25},{2,10},{3,27},{4,12},{5,29},{6,14},{7,31},{8,16},{9,1... | collective-permute-start | bytes 3538952 | tf_op jit(solution)/shard_map/ppermute | solution.py:283
  115.9 17.4 %collective-permute-start.15 = (bf16[512,1152]{1,0:T(8,128)(2,1)S(1)}, bf16[512,1152]{1,0:T(8,128)(2,1)S(1)}, u32[]{:S(2)}, u32[]{:S(2)}) collective-permute-start(bf16[512,1152]{1,0:T(8,128)(2,1)S(1)} %get-tuple-element.82), channel_id=1, source_target_pairs={{0,32},{1,97},{2,34},{3,99},{4,36},{5,101},{6,38},{7,103},{8,40},{... | collective-permute-start | bytes 3538952 | tf_op jit(solution)/shard_map/ppermute | solution.py:283
  117.9 15.4 %collective-permute-start.17 = (bf16[64,4096]{1,0:T(8,128)(2,1)S(1)}, bf16[64,4096]{1,0:T(8,128)(2,1)S(1)}, u32[]{:S(2)}, u32[]{:S(2)}) collective-permute-start(bf16[64,4096]{1,0:T(8,128)(2,1)S(1)} %get-tuple-element.86), channel_id=1, source_target_pairs={{0,2},{1,7},{2,4},{3,1},{4,6},{5,3},{6,0},{7,5},{8,10},{9,15},{10,... | collective-permute-start | bytes 1572872 | tf_op jit(solution)/shard_map/ppermute | solution.py:275
  135.7 17.5 %collective-permute-start.19 = (bf16[512,1152]{1,0:T(8,128)(2,1)S(1)}, bf16[512,1152]{1,0:T(8,128)(2,1)S(1)}, u32[]{:S(2)}, u32[]{:S(2)}) collective-permute-start(bf16[512,1152]{1,0:T(8,128)(2,1)S(1)} %get-tuple-element.90), channel_id=1, source_target_pairs={{0,8},{1,25},{2,10},{3,27},{4,12},{5,29},{6,14},{7,31},{8,16},{9,1... | collective-permute-start | bytes 3538952 | tf_op jit(solution)/shard_map/ppermute | solution.py:283
  135.7 17.4 %collective-permute-start.18 = (bf16[512,1152]{1,0:T(8,128)(2,1)S(1)}, bf16[512,1152]{1,0:T(8,128)(2,1)S(1)}, u32[]{:S(2)}, u32[]{:S(2)}) collective-permute-start(bf16[512,1152]{1,0:T(8,128)(2,1)S(1)} %get-tuple-element.89), channel_id=1, source_target_pairs={{0,32},{1,97},{2,34},{3,99},{4,36},{5,101},{6,38},{7,103},{8,40},{... | collective-permute-start | bytes 3538952 | tf_op jit(solution)/shard_map/ppermute | solution.py:283
  138.8 12.8 %collective-permute-start.20 = (bf16[64,4096]{1,0:T(8,128)(2,1)S(1)}, bf16[64,4096]{1,0:T(8,128)(2,1)S(1)}, u32[]{:S(2)}, u32[]{:S(2)}) collective-permute-start(bf16[64,4096]{1,0:T(8,128)(2,1)S(1)} %row_2.1), channel_id=1, source_target_pairs={{0,2},{1,7},{2,4},{3,1},{4,6},{5,3},{6,0},{7,5},{8,10},{9,15},{10,... | collective-permute-start | bytes 1572872 | tf_op jit(solution)/shard_map/ppermute | solution.py:275
  155.5 10.2 %collective-permute-start.22 = (bf16[128,1152]{1,0:T(8,128)(2,1)S(1)}, bf16[128,1152]{1,0:T(8,128)(2,1)S(1)}, u32[]{:S(2)}, u32[]{:S(2)}) collective-permute-start(bf16[128,1152]{1,0:T(8,128)(2,1)S(1)} %get-tuple-element.97), channel_id=1, source_target_pairs={{0,16},{8,24},{16,0},{24,8},{32,48},{40,56},{48,32},{56,40},{64,80... | collective-permute-start | bytes 884744 | tf_op jit(solution)/shard_map/ppermute | solution.py:268
  157.9 12.3 %collective-permute-start.23 = (bf16[128,1152]{1,0:T(8,128)(2,1)S(1)}, bf16[128,1152]{1,0:T(8,128)(2,1)S(1)}, u32[]{:S(2)}, u32[]{:S(2)}) collective-permute-start(bf16[128,1152]{1,0:T(8,128)(2,1)S(1)} %get-tuple-element.98), channel_id=1, source_target_pairs={{0,24},{8,0},{16,8},{24,16},{32,56},{40,32},{48,40},{56,48},{64,88... | collective-permute-start | bytes 884744 | tf_op jit(solution)/shard_map/ppermute | solution.py:268
  158.2 21.9 %collective-permute-start.27 = (bf16[64,4096]{1,0:T(8,128)(2,1)S(1)}, bf16[64,4096]{1,0:T(8,128)(2,1)S(1)}, u32[]{:S(2)}, u32[]{:S(2)}) collective-permute-start(bf16[64,4096]{1,0:T(8,128)(2,1)S(1)} %row_3.1), channel_id=1, source_target_pairs={{0,2},{1,7},{2,4},{3,1},{4,6},{5,3},{6,0},{7,5},{8,10},{9,15},{10,... | collective-permute-start | bytes 1572872 | tf_op jit(solution)/shard_map/ppermute | solution.py:275
  158.5 13.5 %collective-permute-start.24 = (bf16[128,1152]{1,0:T(8,128)(2,1)S(1)}, bf16[128,1152]{1,0:T(8,128)(2,1)S(1)}, u32[]{:S(2)}, u32[]{:S(2)}) collective-permute-start(bf16[128,1152]{1,0:T(8,128)(2,1)S(1)} %get-tuple-element.99), channel_id=1, source_target_pairs={{0,32},{8,40},{16,48},{24,56},{32,64},{40,72},{48,80},{56,88},{64,... | collective-permute-start | bytes 884744 | tf_op jit(solution)/shard_map/ppermute | solution.py:268
  161.5 11.5 %collective-permute-start.25 = (bf16[128,1152]{1,0:T(8,128)(2,1)S(1)}, bf16[128,1152]{1,0:T(8,128)(2,1)S(1)}, u32[]{:S(2)}, u32[]{:S(2)}) collective-permute-start(bf16[128,1152]{1,0:T(8,128)(2,1)S(1)} %get-tuple-element.100), channel_id=1, source_target_pairs={{0,64},{8,72},{16,80},{24,88},{32,96},{40,104},{48,112},{56,120},{... | collective-permute-start | bytes 884744 | tf_op jit(solution)/shard_map/ppermute | solution.py:268
  165.7 11.3 %collective-permute-start.26 = (bf16[128,1152]{1,0:T(8,128)(2,1)S(1)}, bf16[128,1152]{1,0:T(8,128)(2,1)S(1)}, u32[]{:S(2)}, u32[]{:S(2)}) collective-permute-start(bf16[128,1152]{1,0:T(8,128)(2,1)S(1)} %get-tuple-element.101), channel_id=1, source_target_pairs={{0,96},{8,104},{16,112},{24,120},{32,0},{40,8},{48,16},{56,24},{64... | collective-permute-start | bytes 884744 | tf_op jit(solution)/shard_map/ppermute | solution.py:268
  170.2 9.8 %collective-permute-start.21 = (bf16[128,1152]{1,0:T(8,128)(2,1)S(1)}, bf16[128,1152]{1,0:T(8,128)(2,1)S(1)}, u32[]{:S(2)}, u32[]{:S(2)}) collective-permute-start(bf16[128,1152]{1,0:T(8,128)(2,1)S(1)} %get-tuple-element.96), channel_id=1, source_target_pairs={{0,8},{8,16},{16,24},{24,0},{32,40},{40,48},{48,56},{56,32},{64,72... | collective-permute-start | bytes 884744 | tf_op jit(solution)/shard_map/ppermute | solution.py:268
  180.9 7.8 %collective-permute-start.28 = (bf16[128,1152]{1,0:T(8,128)(2,1)S(1)}, bf16[128,1152]{1,0:T(8,128)(2,1)S(1)}, u32[]{:S(2)}, u32[]{:S(2)}) collective-permute-start(bf16[128,1152]{1,0:T(8,128)(2,1)S(1)} %get-tuple-element.115), channel_id=1, source_target_pairs={{0,128},{8,136},{16,144},{24,152},{32,160},{40,168},{48,176},{56,1... | collective-permute-start | bytes 884744 | tf_op jit(solution)/shard_map/ppermute | solution.py:268
  (21 other events, 55.1 us)

commit v2 on v1

--- a/solution.py
+++ b/solution.py
@@ -241,15 +241,22 @@
     out[...] = ((stay[...] + came[...].astype(F32)) / tokens).astype(BF16)
 
 
-def row_out_kernel(pair, came, out):
-    out[...] = (pair[...] + came[...].astype(F32)).astype(BF16)
-
-
-def pair_kernel(k0, k1, k2, k3, swapped, *outs):
+def pair_kernel(where, k0, k1, k2, k3, swapped, own, stay, far, near):
     half = k0.shape[0]
-    for s, keep in enumerate((k0, k1, k2, k3)):
-        total = keep[...] + swapped[s * half : (s + 1) * half, :].astype(F32)
-        outs[s][...] = total.astype(outs[s].dtype)
+    term = [keep[...] + swapped[s * half : (s + 1) * half, :].astype(F32) for s, keep in enumerate((k0, k1, k2, k3))]
+    even = where[3] % 2 == 0
+    own[...] = term[0]
+    stay[...] = jnp.where(even, term[1], term[3])
+    far[...] = term[2].astype(BF16)
+    near[...] = jnp.where(even, term[3], term[1]).astype(BF16)
+
+
+def row_mid_kernel(stay, came, send):
+    send[...] = (stay[...] + came[...].astype(F32)).astype(BF16)
+
+
+def row_out_kernel(own, near, end, out):
+    out[...] = (own[...] + near[...].astype(F32) + end[...].astype(F32)).astype(BF16)
 
 
 def on_device(hidden, adapter, teacher_rows, scale_exps, packing):
@@ -289,6 +296,8 @@
     x_across, y_across = over_dp(lambda a, b, c: (a, b + 2, c)), over_dp(lambda a, b, c: (a, b, c + 2))
     z_swap = over_dp(lambda a, b, c: (a + 1, b, c))
     core_swap = over_tensor(lambda a, b: (a, b + 1))
+    row_near = over_tensor(lambda a, b: (a ^ 1 if b == 0 else 3 - a, b))
+    row_far = over_tensor(lambda a, b: (3 - a if b == 0 else a ^ 1, b))
     chain = over_tensor(lambda a, b: (a + 1 - 2 * b, b))
 
     where = jnp.stack([zl, x, y, zh, core]).astype(jnp.int32)
@@ -297,24 +306,25 @@
     lanes = width + META
     packing, scale_exps = packing.reshape(1, tok), scale_exps.reshape(1, tok)
 
-    own = [hidden, chain(hidden)]
     squares = light(squares_kernel, "squares", (row,), 10, scale_exps, teacher_rows)[0]
     squares = light(sum_kernel, "pair_squares", (row,), 4, squares, core_swap(squares))[0]
     others = [over_tensor(lambda a, b, k=k: (a + k, b))(squares) for k in (1, 2, 3)]
+    own = [hidden, chain(hidden)]
+    own[1], *others = lax.optimization_barrier((own[1], *others))
     half_rows = jax.ShapeDtypeStruct((tok // 2, lanes), BF16)
     keep, leave = light(
         functools.partial(pack_kernel, share), "pack", (half_rows, half_rows), 18,
         where, packing, scale_exps, squares, *others, teacher_rows, scalars=1,
     )
-    own[1], keep = lax.optimization_barrier((own[1], keep))
     came = z_swap(leave)
     own.append(chain(own[1]))
     sib = [core_swap(block) for block in own]
-    projected = [project_call(own[s], sib[s], adapter) for s in range(2)]
-    came, *projected = lax.optimization_barrier((came, *projected))
+    projected = [project_call(own[s], sib[s], adapter) for s in range(3)]
+    came, *projected[:2] = lax.optimization_barrier((came, *projected[:2]))
     own.append(chain(own[2]))
+    own[3], projected[2] = lax.optimization_barrier((own[3], projected[2]))
     sib.append(core_swap(own[3]))
-    projected += [project_call(own[s], sib[s], adapter) for s in range(2, 4)]
+    projected.append(project_call(own[3], sib[3], adapter))
     merged = light(
         functools.partial(merge_kernel, share), "merge",
         (jax.ShapeDtypeStruct((peers // 2, 2 * share, lanes), BF16),), 10, keep, came,
@@ -344,19 +354,19 @@
     block = jax.ShapeDtypeStruct((half, hidden.shape[1]), F32)
     block16 = jax.ShapeDtypeStruct(block.shape, BF16)
     swapped, _ = lax.optimization_barrier((swapped, ring_a))
-    pair = light(pair_kernel, "pair", (block, block16, block, block), 14, *keeps, swapped)
-    total = chain(pair[1])
-    *came, total = lax.optimization_barrier((*came, total))
+    own_rows, stay, far, near = light(
+        pair_kernel, "pair", (block, block, block16, block16), 18, where, *keeps, swapped, scalars=1
+    )
+    mid = row_near(far)
+    *came, mid = lax.optimization_barrier((*came, mid))
     ring_a, ring_b = weight_call(1, where, held, delta, came)
     came = (x_ring(ring_a), y_ring(ring_b))
-    total, _ = lax.optimization_barrier((total, ring_a))
-    total = chain(light(row_out_kernel, "row_2", (block16,), 8, pair[2], total)[0])
-    *came, total = lax.optimization_barrier((*came, total))
+    mid, near, _ = lax.optimization_barrier((mid, near, ring_a))
+    near = row_near(near)
+    end = row_far(light(row_mid_kernel, "row_mid", (block16,), 8, stay, mid)[0])
+    *came, near, end = lax.optimization_barrier((*came, near, end))
     own_a, a1, a2, a3, own_b, b1, b2, b3 = weight_call(0, where, held, delta, came)
-    total, _ = lax.optimization_barrier((total, a1))
-    total = chain(light(row_out_kernel, "row_3", (block16,), 8, pair[3], total)[0])
     came = (y_forth(a1), y_across(a2), y_back(a3), x_forth(b1), x_across(b2), x_back(b3))
-    *came, total = lax.optimization_barrier((*came, total))
     part = jax.ShapeDtypeStruct((128, width), F32)
     part16 = jax.ShapeDtypeStruct((128, width), BF16)
     stay, leave = light(
@@ -365,7 +375,7 @@
     weight_grad = light(
         functools.partial(weight_out_kernel, tok), "weight_out", (part16,), 8, stay, z_swap(leave)
     )[0]
-    row_grad = light(row_out_kernel, "row_0", (block16,), 8, pair[0], total)[0]
+    row_grad = light(row_out_kernel, "row_out", (block16,), 8, own_rows, near, end)[0]
     return row_grad, weight_grad
 
 

time: 190 us -> 196 us (1.032)
  waiting for transfers between devices: 91.8 us -> 94.8 us
    ppermute x15, waiting for transfers between devices: 37.2 us -> 40.6 us  [over_tensor(): return lambda value: lax.ppermute(value, 'tensor', pairs)]
    ppermute x6, waiting for transfers between devices: 21.2 us -> 18.5 us  [by_core(): return lambda value: lax.ppermute(value, ('dp', 'tensor'), pairs)]
    ppermute x8, waiting for transfers between devices: 33.5 us -> 35.7 us  [over_dp(): return lambda value: lax.ppermute(value, 'dp', pairs)]
    pallas_call x12 -> x11, Pallas kernels: 8.67 us -> 9.28 us  [light(): pl.pallas_call(kernel, out_shape=tuple(out_shape), in_specs=[pl.BlockSpec...]
  transfers between devices with their start and end apart: 30 -> 30, of which waited for: 16 -> 15; matrix products, arithmetic and copies ran while one was open for 0% -> 0% of each run, Pallas kernels for 14% -> 13%
where the time goes in v2:
time: 196 us
  waiting for transfers between devices  94.8 us (48%)
  Pallas kernels  38.9 us (20%)
  starting transfers between devices  38.7 us (20%)
  local copies, waits for them, and re-layouts  22.4 us (11%)
    ppermute x15, waiting for transfers between devices, over_tensor(): return lambda value: lax.ppermute(value, 'tensor', pairs)  40.6 us
    ppermute x8, waiting for transfers between devices, over_dp(): return lambda value: lax.ppermute(value, 'dp', pairs)  35.7 us
    unnamed x46, local copies, waits for them, and re-layouts  22.4 us
    ppermute x6, waiting for transfers between devices, by_core(): return lambda value: lax.ppermute(value, ('dp', 'tensor'), pairs)  18.5 us
    ppermute x15, starting transfers between devices, over_tensor(): return lambda value: lax.ppermute(value, 'tensor', pairs)  16.9 us
    pallas_call x4, Pallas kernels, project_call(): pl.pallas_call(project_kernel, out_shape=jax.ShapeDtypeStruct((2 * half,...  12.6 us
    pallas_call x4, Pallas kernels, weight_call(): pl.pallas_call(functools.partial(weight_kernel, k, len(came) > 0, turn),...  9.48 us
    pallas_call x11, Pallas kernels, light(): pl.pallas_call(kernel, out_shape=tuple(out_shape), in_specs=[pl.BlockSpec...  9.28 us
  transfers between devices with their start and end apart: 30, of which 15 were waited for; matrix products, arithmetic and copies ran while one was open for 0% of the time, Pallas kernels for 13%

profile of v2, /device:TPU:6, one launch (start us, length us, event | category | flops | bytes accessed | tf_op | source)
XLA Modules:
  0.0 195.7 jit_solution(17294759656857314737)
XLA Ops:
  0.6 3.3 %collective-permute-start.1 = (bf16[64,4096]{1,0:T(8,128)(2,1)}, bf16[64,4096]{1,0:T(8,128)(2,1)S(1)}, u32[]{:S(2)}, u32[]{:S(2)}) collective-permute-start(bf16[64,4096]{1,0:T(8,128)(2,1)} %refs_0_.7), channel_id=1, source_target_pairs={{0,2},{1,7},{2,4},{3,1},{4,6},{5,3},{6,0},{7,5},{8,10},{9,15},{10,... | collective-permute-start | bytes 1572872 | tf_op jit(solution)/shard_map/ppermute | solution.py:282
  6.3 2.7 %collective-permute-start = (f32[1,512]{1,0:T(1,128)S(1)}, f32[1,512]{1,0:T(1,128)S(1)}, u32[]{:S(2)}, u32[]{:S(2)}) collective-permute-start(f32[1,512]{1,0:T(1,128)S(1)} %squares.1.refs_0_), channel_id=1, source_target_pairs={{0,1},{1,0},{2,3},{3,2},{4,5},{5,4},{6,7},{7,6},{8,9},{9,8},{10,11... | collective-permute-start | bytes 6152 | tf_op jit(solution)/shard_map/ppermute | solution.py:282
  11.2 4.4 %collective-permute-start.3 = (f32[1,512]{1,0:T(1,128)S(1)}, f32[1,512]{1,0:T(1,128)S(1)}, u32[]{:S(2)}, u32[]{:S(2)}) collective-permute-start(f32[1,512]{1,0:T(1,128)S(1)} %pair_squares.1.s0_ref), channel_id=1, source_target_pairs={{0,4},{1,5},{2,6},{3,7},{4,0},{5,1},{6,2},{7,3},{8,12},{9,13},{10,... | collective-permute-start | bytes 6152 | tf_op jit(solution)/shard_map/ppermute | solution.py:282
  15.9 6.6 %collective-permute-done.3.s2_ref = f32[1,512]{1,0:T(1,128)S(1)} collective-permute-done((f32[1,512]{1,0:T(1,128)S(1)}, f32[1,512]{1,0:T(1,128)S(1)}, u32[]{:S(2)}, u32[]{:S(2)}) %collective-permute-start.3) | collective-permute-done | bytes 2080 | tf_op jit(solution)/shard_map/ppermute | solution.py:282
  23.8 1.8 pack.1
  27.8 3.7 %copy-done = bf16[4096,1152]{1,0:T(8,128)(2,1)S(1)} copy-done((bf16[4096,1152]{1,0:T(8,128)(2,1)S(1)}, bf16[4096,1152]{1,0:T(8,128)(2,1)}, u32[]{:S(2)}) %copy-start) | copy-done | bytes 9437208
  31.4 3.2 %project.4.p0_ref = f32[128,1152]{1,0:T(8,128)S(1)} custom-call(bf16[64,4096]{1,0:T(8,128)(2,1)S(1)} %copy-done.4, bf16[64,4096]{1,0:T(8,128)(2,1)S(1)} %collective-permute-done.6.sib_ref.refs_1_, bf16[4096,1152]{1,0:T(8,128)(2,1)S(1)} %copy-done), custom_call_target="tpu_custom_call" | custom-call | tf_op jit(solution)/shard_map/project/pallas_call | solution.py:111
  35.1 3.2 %project.5.p1_ref = f32[128,1152]{1,0:T(8,128)S(1)} custom-call(bf16[64,4096]{1,0:T(8,128)(2,1)S(1)} %collective-permute-done.1.own_ref.refs_2_, bf16[64,4096]{1,0:T(8,128)(2,1)S(1)} %collective-permute-done.7.sib_ref.refs_3_, bf16[4096,1152]{1,0:T(8,128)(2,1)S(1)} %copy-done.1), custom_call_target="tpu_custom_call" | custom-call | tf_op jit(solution)/shard_map/project/pallas_call | solution.py:111
  39.1 9.9 %collective-permute-done.5.came_ref = bf16[256,1280]{1,0:T(8,128)(2,1)S(1)} collective-permute-done((bf16[256,1280]{1,0:T(8,128)(2,1)S(1)}, bf16[256,1280]{1,0:T(8,128)(2,1)S(1)}, u32[]{:S(2)}, u32[]{:S(2)}) %collective-permute-start.5) | collective-permute-done | bytes 655392 | tf_op jit(solution)/shard_map/ppermute | solution.py:275
  50.2 7.4 %all-to-all-start = ((bf16[16,32,1280]{2,1,0:T(8,128)(2,1)}), bf16[16,32,1280]{2,1,0:T(8,128)(2,1)}, u32[]{:S(2)}, u32[]{:S(2)}) async-start(bf16[16,32,1280]{2,1,0:T(8,128)(2,1)} %copy-done.9), calls=%async_computation | async-start | bytes 2621440 | tf_op jit(solution)/shard_map/all_to_all | solution.py:333
  59.6 3.7 %copy-done.2 = bf16[4096,1152]{1,0:T(8,128)(2,1)S(1)} copy-done((bf16[4096,1152]{1,0:T(8,128)(2,1)S(1)}, bf16[4096,1152]{1,0:T(8,128)(2,1)}, u32[]{:S(2)}) %copy-start.2) | copy-done | bytes 9437208
  63.3 3.2 %project.6.p2_ref = f32[128,1152]{1,0:T(8,128)S(1)} custom-call(bf16[64,4096]{1,0:T(8,128)(2,1)S(1)} %collective-permute-done.8.own_ref.refs_4_, bf16[64,4096]{1,0:T(8,128)(2,1)S(1)} %collective-permute-done.10.sib_ref.refs_5_, bf16[4096,1152]{1,0:T(8,128)(2,1)S(1)} %copy-done.2), custom_call_target="tpu_custom_call" | custom-call | tf_op jit(solution)/shard_map/project/pallas_call | solution.py:111
  67.3 6.5 %collective-permute-done.9.own_ref.refs_6_ = bf16[64,4096]{1,0:T(8,128)(2,1)S(1)} collective-permute-done((bf16[64,4096]{1,0:T(8,128)(2,1)S(1)}, bf16[64,4096]{1,0:T(8,128)(2,1)S(1)}, u32[]{:S(2)}, u32[]{:S(2)}) %collective-permute-start.9) | collective-permute-done | bytes 524320 | tf_op jit(solution)/shard_map/ppermute | solution.py:282
  73.8 1.9 collective-permute-done.11.sib_ref.refs_7_
  75.7 3.2 %project.7.p3_ref = f32[128,1152]{1,0:T(8,128)S(1)} custom-call(bf16[64,4096]{1,0:T(8,128)(2,1)S(1)} %collective-permute-done.9.own_ref.refs_6_, bf16[64,4096]{1,0:T(8,128)(2,1)S(1)} %collective-permute-done.11.sib_ref.refs_7_, bf16[4096,1152]{1,0:T(8,128)(2,1)S(1)} %copy-done.2), custom_call_target="tpu_custom_call" | custom-call | tf_op jit(solution)/shard_map/project/pallas_call | solution.py:111
  81.3 2.5 %place.1 = (bf16[512,1152]{1,0:T(8,128)(2,1)S(1)}, f32[512,128]{1,0:T(8,128)S(1)}) custom-call(bf16[512,1280]{1,0:T(8,128)(2,1)} %bitcast.7.got_ref), custom_call_target="tpu_custom_call" | custom-call | tf_op jit(solution)/shard_map/place/pallas_call | solution.py:221
  87.1 2.3 %weight_3.1 = (bf16[512,1152]{1,0:T(8,128)(2,1)S(1)}, bf16[512,1152]{1,0:T(8,128)(2,1)S(1)}) custom-call(s32[5]{0:T(128)S(1)} %stack.23.where_ref.where, bf16[64,4096]{1,0:T(8,128)(2,1)S(1)} %copy-done.4, bf16[64,4096]{1,0:T(8,128)(2,1)S(1)} %collective-permute-done.6.sib_ref.refs_1_, bf16[64,4096]{1,0:T(8,128)(2,1)S(1)} %collective-permute-done.1.own_ref.refs_2_, ...), custom_call_target="tpu_custom_call" | custom-call | tf_op jit(solution)/shard_map/weight_3/pallas_call | solution.py:207
  91.6 3.7 %copy-done.3 = bf16[4096,1152]{1,0:T(8,128)(2,1)S(1)} copy-done((bf16[4096,1152]{1,0:T(8,128)(2,1)S(1)}, bf16[4096,1152]{1,0:T(8,128)(2,1)}, u32[]{:S(2)}) %copy-start.3) | copy-done | bytes 9437208
  95.2 7.5 %row_terms.1 = (f32[64,4096]{1,0:T(8,128)S(1)}, f32[64,4096]{1,0:T(8,128)S(1)}, f32[64,4096]{1,0:T(8,128)S(1)}, f32[64,4096]{1,0:T(8,128)S(1)}, bf16[256,4096]{1,0:T(8,128)(2,1)S(1)}) custom-call(bf16[512,1152]{1,0:T(8,128)(2,1)S(1)} %delta.1.refs_8_.delta_ref, bf16[4096,1152]{1,0:T(8,128)(2,1)S(1)} %copy-done.3), custom_call_target="tpu_custom_call" | custom-call | tf_op jit(solution)/shard_map/row_terms/pallas_call | solution.py:155
  102.7 4.3 %collective-permute-done.13.refs_10_ = bf16[512,1152]{1,0:T(8,128)(2,1)S(1)} collective-permute-done((bf16[512,1152]{1,0:T(8,128)(2,1)S(1)}, bf16[512,1152]{1,0:T(8,128)(2,1)S(1)}, u32[]{:S(2)}, u32[]{:S(2)}) %collective-permute-start.13) | collective-permute-done | bytes 1179680 | tf_op jit(solution)/shard_map/ppermute | solution.py:290
  108.3 2.4 %weight_2.1 = (bf16[512,1152]{1,0:T(8,128)(2,1)S(1)}, bf16[512,1152]{1,0:T(8,128)(2,1)S(1)}) custom-call(s32[5]{0:T(128)S(1)} %stack.23.where_ref.where, bf16[64,4096]{1,0:T(8,128)(2,1)S(1)} %copy-done.4, bf16[64,4096]{1,0:T(8,128)(2,1)S(1)} %collective-permute-done.6.sib_ref.refs_1_, bf16[64,4096]{1,0:T(8,128)(2,1)S(1)} %collective-permute-done.1.own_ref.refs_2_, ...), custom_call_target="tpu_custom_call" | custom-call | tf_op jit(solution)/shard_map/weight_2/pallas_call | solution.py:207
  114.2 14.0 %collective-permute-done.16.refs_10_ = bf16[512,1152]{1,0:T(8,128)(2,1)S(1)} collective-permute-done((bf16[512,1152]{1,0:T(8,128)(2,1)S(1)}, bf16[512,1152]{1,0:T(8,128)(2,1)S(1)}, u32[]{:S(2)}, u32[]{:S(2)}) %collective-permute-start.16) | collective-permute-done | bytes 1179680 | tf_op jit(solution)/shard_map/ppermute | solution.py:290
  128.2 2.4 %weight_1.1 = (bf16[512,1152]{1,0:T(8,128)(2,1)S(1)}, bf16[512,1152]{1,0:T(8,128)(2,1)S(1)}) custom-call(s32[5]{0:T(128)S(1)} %stack.23.where_ref.where, bf16[64,4096]{1,0:T(8,128)(2,1)S(1)} %copy-done.4, bf16[64,4096]{1,0:T(8,128)(2,1)S(1)} %collective-permute-done.6.sib_ref.refs_1_, bf16[64,4096]{1,0:T(8,128)(2,1)S(1)} %collective-permute-done.1.own_ref.refs_2_, ...), custom_call_target="tpu_custom_call" | custom-call | tf_op jit(solution)/shard_map/weight_1/pallas_call | solution.py:207
  131.0 3.0 %collective-permute-start.18 = (bf16[512,1152]{1,0:T(8,128)(2,1)S(1)}, bf16[512,1152]{1,0:T(8,128)(2,1)S(1)}, u32[]{:S(2)}, u32[]{:S(2)}) collective-permute-start(bf16[512,1152]{1,0:T(8,128)(2,1)S(1)} %get-tuple-element.91), channel_id=1, source_target_pairs={{0,32},{1,97},{2,34},{3,99},{4,36},{5,101},{6,38},{7,103},{8,40},{... | collective-permute-start | bytes 3538952 | tf_op jit(solution)/shard_map/ppermute | solution.py:290
  134.1 2.5 %collective-permute-start.21 = (bf16[64,4096]{1,0:T(8,128)(2,1)S(1)}, bf16[64,4096]{1,0:T(8,128)(2,1)S(1)}, u32[]{:S(2)}, u32[]{:S(2)}) collective-permute-start(bf16[64,4096]{1,0:T(8,128)(2,1)S(1)} %row_mid.1), channel_id=1, source_target_pairs={{0,6},{1,3},{2,4},{3,1},{4,2},{5,7},{6,0},{7,5},{8,14},{9,11},{10,... | collective-permute-start | bytes 1572872 | tf_op jit(solution)/shard_map/ppermute | solution.py:282
  136.5 21.8 %collective-permute-done.20.near = bf16[64,4096]{1,0:T(8,128)(2,1)S(1)} collective-permute-done((bf16[64,4096]{1,0:T(8,128)(2,1)S(1)}, bf16[64,4096]{1,0:T(8,128)(2,1)S(1)}, u32[]{:S(2)}, u32[]{:S(2)}) %collective-permute-start.20) | collective-permute-done | bytes 524320 | tf_op jit(solution)/shard_map/ppermute | solution.py:282
  158.4 2.4 %weight_0.1 = (f32[128,1152]{1,0:T(8,128)S(1)}, bf16[128,1152]{1,0:T(8,128)(2,1)S(1)}, bf16[128,1152]{1,0:T(8,128)(2,1)S(1)}, bf16[128,1152]{1,0:T(8,128)(2,1)S(...) custom-call(s32[5]{0:T(128)S(1)} %stack.23.where_ref.where, ...), custom_call_target="tpu_custom_call" | custom-call | tf_op jit(solution)/shard_map/weight_0/pallas_call | solution.py:207
  160.9 2.7 %collective-permute-start.23 = (bf16[128,1152]{1,0:T(8,128)(2,1)S(1)}, bf16[128,1152]{1,0:T(8,128)(2,1)S(1)}, u32[]{:S(2)}, u32[]{:S(2)}) collective-permute-start(bf16[128,1152]{1,0:T(8,128)(2,1)S(1)} %get-tuple-element.104), channel_id=1, source_target_pairs={{0,16},{8,24},{16,0},{24,8},{32,48},{40,56},{48,32},{56,40},{64,80... | collective-permute-start | bytes 884744 | tf_op jit(solution)/shard_map/ppermute | solution.py:275
  165.2 2.0 %collective-permute-start.26 = (bf16[128,1152]{1,0:T(8,128)(2,1)S(1)}, bf16[128,1152]{1,0:T(8,128)(2,1)S(1)}, u32[]{:S(2)}, u32[]{:S(2)}) collective-permute-start(bf16[128,1152]{1,0:T(8,128)(2,1)S(1)} %get-tuple-element.108), channel_id=1, source_target_pairs={{0,64},{8,72},{16,80},{24,88},{32,96},{40,104},{48,112},{56,120},{... | collective-permute-start | bytes 884744 | tf_op jit(solution)/shard_map/ppermute | solution.py:275
  167.2 9.8 %collective-permute-done.22.a1 = bf16[128,1152]{1,0:T(8,128)(2,1)S(1)} collective-permute-done((bf16[128,1152]{1,0:T(8,128)(2,1)S(1)}, bf16[128,1152]{1,0:T(8,128)(2,1)S(1)}, u32[]{:S(2)}, u32[]{:S(2)}) %collective-permute-start.22) | collective-permute-done | bytes 294944 | tf_op jit(solution)/shard_map/ppermute | solution.py:275
  177.6 8.9 %collective-permute-done.27.b3 = bf16[128,1152]{1,0:T(8,128)(2,1)S(1)} collective-permute-done((bf16[128,1152]{1,0:T(8,128)(2,1)S(1)}, bf16[128,1152]{1,0:T(8,128)(2,1)S(1)}, u32[]{:S(2)}, u32[]{:S(2)}) %collective-permute-start.27) | collective-permute-done | bytes 294944 | tf_op jit(solution)/shard_map/ppermute | solution.py:275
  188.5 6.4 %collective-permute-done.28.came = bf16[128,1152]{1,0:T(8,128)(2,1)S(1)} collective-permute-done((bf16[128,1152]{1,0:T(8,128)(2,1)S(1)}, bf16[128,1152]{1,0:T(8,128)(2,1)S(1)}, u32[]{:S(2)}, u32[]{:S(2)}) %collective-permute-start.28) | collective-permute-done | bytes 294944 | tf_op jit(solution)/shard_map/ppermute | solution.py:275
  (95 shorter events, 31.8 us)
Async XLA Ops:
  0.6 21.9 %collective-permute-start.1 = (bf16[64,4096]{1,0:T(8,128)(2,1)}, bf16[64,4096]{1,0:T(8,128)(2,1)S(1)}, u32[]{:S(2)}, u32[]{:S(2)}) collective-permute-start(bf16[64,4096]{1,0:T(8,128)(2,1)} %refs_0_.7), channel_id=1, source_target_pairs={{0,2},{1,7},{2,4},{3,1},{4,6},{5,3},{6,0},{7,5},{8,10},{9,15},{10,... | collective-permute-start | bytes 1572872 | tf_op jit(solution)/shard_map/ppermute | solution.py:282
  5.9 16.6 %copy-start.22 = (s32[512]{0:T(512)S(1)}, s32[512]{0:T(512)}, u32[]{:S(2)}) copy-start(s32[512]{0:T(512)} %param.9) | copy-start | bytes 6148
  5.9 19.8 %copy-start.4 = (bf16[64,4096]{1,0:T(8,128)(2,1)S(1)}, bf16[64,4096]{1,0:T(8,128)(2,1)}, u32[]{:S(2)}) copy-start(bf16[64,4096]{1,0:T(8,128)(2,1)} %refs_0_.7) | copy-start | bytes 1572868
  6.3 3.5 %collective-permute-start = (f32[1,512]{1,0:T(1,128)S(1)}, f32[1,512]{1,0:T(1,128)S(1)}, u32[]{:S(2)}, u32[]{:S(2)}) collective-permute-start(f32[1,512]{1,0:T(1,128)S(1)} %squares.1.refs_0_), channel_id=1, source_target_pairs={{0,1},{1,0},{2,3},{3,2},{4,5},{5,4},{6,7},{7,6},{8,9},{9,8},{10,11... | collective-permute-start | bytes 6152 | tf_op jit(solution)/shard_map/ppermute | solution.py:282
  9.7 6.2 %collective-permute-start.4 = (f32[1,512]{1,0:T(1,128)S(1)}, f32[1,512]{1,0:T(1,128)S(1)}, u32[]{:S(2)}, u32[]{:S(2)}) collective-permute-start(f32[1,512]{1,0:T(1,128)S(1)} %pair_squares.1.s0_ref), channel_id=1, source_target_pairs={{0,6},{1,7},{2,0},{3,1},{4,2},{5,3},{6,4},{7,5},{8,14},{9,15},{10,... | collective-permute-start | bytes 6152 | tf_op jit(solution)/shard_map/ppermute | solution.py:282
  11.2 11.3 %collective-permute-start.3 = (f32[1,512]{1,0:T(1,128)S(1)}, f32[1,512]{1,0:T(1,128)S(1)}, u32[]{:S(2)}, u32[]{:S(2)}) collective-permute-start(f32[1,512]{1,0:T(1,128)S(1)} %pair_squares.1.s0_ref), channel_id=1, source_target_pairs={{0,4},{1,5},{2,6},{3,7},{4,0},{5,1},{6,2},{7,3},{8,12},{9,13},{10,... | collective-permute-start | bytes 6152 | tf_op jit(solution)/shard_map/ppermute | solution.py:282
  15.6 7.0 %collective-permute-start.2 = (f32[1,512]{1,0:T(1,128)S(1)}, f32[1,512]{1,0:T(1,128)S(1)}, u32[]{:S(2)}, u32[]{:S(2)}) collective-permute-start(f32[1,512]{1,0:T(1,128)S(1)} %pair_squares.1.s0_ref), channel_id=1, source_target_pairs={{0,2},{1,3},{2,4},{3,5},{4,6},{5,7},{6,0},{7,1},{8,10},{9,11},{10,... | collective-permute-start | bytes 6152 | tf_op jit(solution)/shard_map/ppermute | solution.py:282
  25.7 23.4 %collective-permute-start.5 = (bf16[256,1280]{1,0:T(8,128)(2,1)S(1)}, bf16[256,1280]{1,0:T(8,128)(2,1)S(1)}, u32[]{:S(2)}, u32[]{:S(2)}) collective-permute-start(bf16[256,1280]{1,0:T(8,128)(2,1)S(1)} %get-tuple-element.60), channel_id=1, source_target_pairs={{0,128},{8,136},{16,144},{24,152},{32,160},{40,168},{48,176},{56,1... | collective-permute-start | bytes 1966088 | tf_op jit(solution)/shard_map/ppermute | solution.py:275
  25.8 2.0 %collective-permute-start.6 = (bf16[64,4096]{1,0:T(8,128)(2,1)S(1)}, bf16[64,4096]{1,0:T(8,128)(2,1)S(1)}, u32[]{:S(2)}, u32[]{:S(2)}) collective-permute-start(bf16[64,4096]{1,0:T(8,128)(2,1)S(1)} %copy-done.4), channel_id=1, source_target_pairs={{0,1},{1,0},{2,3},{3,2},{4,5},{5,4},{6,7},{7,6},{8,9},{9,8},{10,11... | collective-permute-start | bytes 1572872 | tf_op jit(solution)/shard_map/ppermute | solution.py:282
  25.9 8.8 %collective-permute-start.7 = (bf16[64,4096]{1,0:T(8,128)(2,1)S(1)}, bf16[64,4096]{1,0:T(8,128)(2,1)S(1)}, u32[]{:S(2)}, u32[]{:S(2)}) collective-permute-start(bf16[64,4096]{1,0:T(8,128)(2,1)S(1)} %collective-permute-done.1.own_ref.refs_2_), channel_id=1, source_target_pairs={{0,1},{1,0},{2,3},{3,2},{4,5},{5,4},{6,7},{7,6},{8,9},{9,8},{10,11... | collective-permute-start | bytes 1572872 | tf_op jit(solution)/shard_map/ppermute | solution.py:282
  26.4 31.3 %collective-permute-start.8 = (bf16[64,4096]{1,0:T(8,128)(2,1)S(1)}, bf16[64,4096]{1,0:T(8,128)(2,1)S(1)}, u32[]{:S(2)}, u32[]{:S(2)}) collective-permute-start(bf16[64,4096]{1,0:T(8,128)(2,1)S(1)} %collective-permute-done.1.own_ref.refs_2_), channel_id=1, source_target_pairs={{0,2},{1,7},{2,4},{3,1},{4,6},{5,3},{6,0},{7,5},{8,10},{9,15},{10,... | collective-permute-start | bytes 1572872 | tf_op jit(solution)/shard_map/ppermute | solution.py:282
  50.2 31.1 %all-to-all-start = ((bf16[16,32,1280]{2,1,0:T(8,128)(2,1)}), bf16[16,32,1280]{2,1,0:T(8,128)(2,1)}, u32[]{:S(2)}, u32[]{:S(2)}) async-start(bf16[16,32,1280]{2,1,0:T(8,128)(2,1)} %copy-done.9), calls=%async_computation | async-start | bytes 2621440 | tf_op jit(solution)/shard_map/all_to_all | solution.py:333
  57.6 2.0 %collective-permute-start.10 = (bf16[64,4096]{1,0:T(8,128)(2,1)S(1)}, bf16[64,4096]{1,0:T(8,128)(2,1)S(1)}, u32[]{:S(2)}, u32[]{:S(2)}) collective-permute-start(bf16[64,4096]{1,0:T(8,128)(2,1)S(1)} %collective-permute-done.8.own_ref.refs_4_), channel_id=1, source_target_pairs={{0,1},{1,0},{2,3},{3,2},{4,5},{5,4},{6,7},{7,6},{8,9},{9,8},{10,11... | collective-permute-start | bytes 1572872 | tf_op jit(solution)/shard_map/ppermute | solution.py:282
  57.7 16.0 %collective-permute-start.9 = (bf16[64,4096]{1,0:T(8,128)(2,1)S(1)}, bf16[64,4096]{1,0:T(8,128)(2,1)S(1)}, u32[]{:S(2)}, u32[]{:S(2)}) collective-permute-start(bf16[64,4096]{1,0:T(8,128)(2,1)S(1)} %collective-permute-done.8.own_ref.refs_4_), channel_id=1, source_target_pairs={{0,2},{1,7},{2,4},{3,1},{4,6},{5,3},{6,0},{7,5},{8,10},{9,15},{10,... | collective-permute-start | bytes 1572872 | tf_op jit(solution)/shard_map/ppermute | solution.py:282
  73.7 1.9 collective-permute-start.11
  89.5 17.5 %collective-permute-start.13 = (bf16[512,1152]{1,0:T(8,128)(2,1)S(1)}, bf16[512,1152]{1,0:T(8,128)(2,1)S(1)}, u32[]{:S(2)}, u32[]{:S(2)}) collective-permute-start(bf16[512,1152]{1,0:T(8,128)(2,1)S(1)} %get-tuple-element.79), channel_id=1, source_target_pairs={{0,8},{1,25},{2,10},{3,27},{4,12},{5,29},{6,14},{7,31},{8,16},{9,1... | collective-permute-start | bytes 3538952 | tf_op jit(solution)/shard_map/ppermute | solution.py:290
  91.0 16.2 %collective-permute-start.12 = (bf16[512,1152]{1,0:T(8,128)(2,1)S(1)}, bf16[512,1152]{1,0:T(8,128)(2,1)S(1)}, u32[]{:S(2)}, u32[]{:S(2)}) collective-permute-start(bf16[512,1152]{1,0:T(8,128)(2,1)S(1)} %get-tuple-element.73), channel_id=1, source_target_pairs={{0,32},{1,97},{2,34},{3,99},{4,36},{5,101},{6,38},{7,103},{8,40},{... | collective-permute-start | bytes 3538952 | tf_op jit(solution)/shard_map/ppermute | solution.py:290
  107.2 5.7 %collective-permute-start.14 = (bf16[256,4096]{1,0:T(8,128)(2,1)S(1)}, bf16[256,4096]{1,0:T(8,128)(2,1)S(1)}, u32[]{:S(2)}, u32[]{:S(2)}) collective-permute-start(bf16[256,4096]{1,0:T(8,128)(2,1)S(1)} %get-tuple-element.81), channel_id=1, source_target_pairs={{0,1},{1,0},{2,3},{3,2},{4,5},{5,4},{6,7},{7,6},{8,9},{9,8},{10,11... | collective-permute-start | bytes 6291464 | tf_op jit(solution)/shard_map/ppermute | solution.py:282
  110.7 17.5 %collective-permute-start.16 = (bf16[512,1152]{1,0:T(8,128)(2,1)S(1)}, bf16[512,1152]{1,0:T(8,128)(2,1)S(1)}, u32[]{:S(2)}, u32[]{:S(2)}) collective-permute-start(bf16[512,1152]{1,0:T(8,128)(2,1)S(1)} %get-tuple-element.87), channel_id=1, source_target_pairs={{0,8},{1,25},{2,10},{3,27},{4,12},{5,29},{6,14},{7,31},{8,16},{9,1... | collective-permute-start | bytes 3538952 | tf_op jit(solution)/shard_map/ppermute | solution.py:290
  111.1 17.1 %collective-permute-start.15 = (bf16[512,1152]{1,0:T(8,128)(2,1)S(1)}, bf16[512,1152]{1,0:T(8,128)(2,1)S(1)}, u32[]{:S(2)}, u32[]{:S(2)}) collective-permute-start(bf16[512,1152]{1,0:T(8,128)(2,1)S(1)} %get-tuple-element.84), channel_id=1, source_target_pairs={{0,32},{1,97},{2,34},{3,99},{4,36},{5,101},{6,38},{7,103},{8,40},{... | collective-permute-start | bytes 3538952 | tf_op jit(solution)/shard_map/ppermute | solution.py:290
  113.9 14.3 %collective-permute-start.17 = (bf16[64,4096]{1,0:T(8,128)(2,1)S(1)}, bf16[64,4096]{1,0:T(8,128)(2,1)S(1)}, u32[]{:S(2)}, u32[]{:S(2)}) collective-permute-start(bf16[64,4096]{1,0:T(8,128)(2,1)S(1)} %get-tuple-element.88), channel_id=1, source_target_pairs={{0,2},{1,7},{2,0},{3,5},{4,6},{5,3},{6,4},{7,1},{8,10},{9,15},{10,... | collective-permute-start | bytes 1572872 | tf_op jit(solution)/shard_map/ppermute | solution.py:282
  130.6 27.7 %collective-permute-start.19 = (bf16[512,1152]{1,0:T(8,128)(2,1)S(1)}, bf16[512,1152]{1,0:T(8,128)(2,1)S(1)}, u32[]{:S(2)}, u32[]{:S(2)}) collective-permute-start(bf16[512,1152]{1,0:T(8,128)(2,1)S(1)} %get-tuple-element.92), channel_id=1, source_target_pairs={{0,8},{1,25},{2,10},{3,27},{4,12},{5,29},{6,14},{7,31},{8,16},{9,1... | collective-permute-start | bytes 3538952 | tf_op jit(solution)/shard_map/ppermute | solution.py:290
  131.0 27.4 %collective-permute-start.18 = (bf16[512,1152]{1,0:T(8,128)(2,1)S(1)}, bf16[512,1152]{1,0:T(8,128)(2,1)S(1)}, u32[]{:S(2)}, u32[]{:S(2)}) collective-permute-start(bf16[512,1152]{1,0:T(8,128)(2,1)S(1)} %get-tuple-element.91), channel_id=1, source_target_pairs={{0,32},{1,97},{2,34},{3,99},{4,36},{5,101},{6,38},{7,103},{8,40},{... | collective-permute-start | bytes 3538952 | tf_op jit(solution)/shard_map/ppermute | solution.py:290
  134.0 24.4 %collective-permute-start.20 = (bf16[64,4096]{1,0:T(8,128)(2,1)S(1)}, bf16[64,4096]{1,0:T(8,128)(2,1)S(1)}, u32[]{:S(2)}, u32[]{:S(2)}) collective-permute-start(bf16[64,4096]{1,0:T(8,128)(2,1)S(1)} %get-tuple-element.95), channel_id=1, source_target_pairs={{0,2},{1,7},{2,0},{3,5},{4,6},{5,3},{6,4},{7,1},{8,10},{9,15},{10,... | collective-permute-start | bytes 1572872 | tf_op jit(solution)/shard_map/ppermute | solution.py:282
  134.1 24.3 %collective-permute-start.21 = (bf16[64,4096]{1,0:T(8,128)(2,1)S(1)}, bf16[64,4096]{1,0:T(8,128)(2,1)S(1)}, u32[]{:S(2)}, u32[]{:S(2)}) collective-permute-start(bf16[64,4096]{1,0:T(8,128)(2,1)S(1)} %row_mid.1), channel_id=1, source_target_pairs={{0,6},{1,3},{2,4},{3,1},{4,2},{5,7},{6,0},{7,5},{8,14},{9,11},{10,... | collective-permute-start | bytes 1572872 | tf_op jit(solution)/shard_map/ppermute | solution.py:282
  160.7 16.3 %collective-permute-start.22 = (bf16[128,1152]{1,0:T(8,128)(2,1)S(1)}, bf16[128,1152]{1,0:T(8,128)(2,1)S(1)}, u32[]{:S(2)}, u32[]{:S(2)}) collective-permute-start(bf16[128,1152]{1,0:T(8,128)(2,1)S(1)} %get-tuple-element.103), channel_id=1, source_target_pairs={{0,8},{8,16},{16,24},{24,0},{32,40},{40,48},{48,56},{56,32},{64,72... | collective-permute-start | bytes 884744 | tf_op jit(solution)/shard_map/ppermute | solution.py:275
  160.9 16.1 %collective-permute-start.23 = (bf16[128,1152]{1,0:T(8,128)(2,1)S(1)}, bf16[128,1152]{1,0:T(8,128)(2,1)S(1)}, u32[]{:S(2)}, u32[]{:S(2)}) collective-permute-start(bf16[128,1152]{1,0:T(8,128)(2,1)S(1)} %get-tuple-element.104), channel_id=1, source_target_pairs={{0,16},{8,24},{16,0},{24,8},{32,48},{40,56},{48,32},{56,40},{64,80... | collective-permute-start | bytes 884744 | tf_op jit(solution)/shard_map/ppermute | solution.py:275
  163.6 14.0 %collective-permute-start.24 = (bf16[128,1152]{1,0:T(8,128)(2,1)S(1)}, bf16[128,1152]{1,0:T(8,128)(2,1)S(1)}, u32[]{:S(2)}, u32[]{:S(2)}) collective-permute-start(bf16[128,1152]{1,0:T(8,128)(2,1)S(1)} %get-tuple-element.105), channel_id=1, source_target_pairs={{0,24},{8,0},{16,8},{24,16},{32,56},{40,32},{48,40},{56,48},{64,88... | collective-permute-start | bytes 884744 | tf_op jit(solution)/shard_map/ppermute | solution.py:275
  164.6 13.0 %collective-permute-start.25 = (bf16[128,1152]{1,0:T(8,128)(2,1)S(1)}, bf16[128,1152]{1,0:T(8,128)(2,1)S(1)}, u32[]{:S(2)}, u32[]{:S(2)}) collective-permute-start(bf16[128,1152]{1,0:T(8,128)(2,1)S(1)} %get-tuple-element.107), channel_id=1, source_target_pairs={{0,32},{8,40},{16,48},{24,56},{32,64},{40,72},{48,80},{56,88},{64,... | collective-permute-start | bytes 884744 | tf_op jit(solution)/shard_map/ppermute | solution.py:275
  165.2 12.5 %collective-permute-start.26 = (bf16[128,1152]{1,0:T(8,128)(2,1)S(1)}, bf16[128,1152]{1,0:T(8,128)(2,1)S(1)}, u32[]{:S(2)}, u32[]{:S(2)}) collective-permute-start(bf16[128,1152]{1,0:T(8,128)(2,1)S(1)} %get-tuple-element.108), channel_id=1, source_target_pairs={{0,64},{8,72},{16,80},{24,88},{32,96},{40,104},{48,112},{56,120},{... | collective-permute-start | bytes 884744 | tf_op jit(solution)/shard_map/ppermute | solution.py:275
  177.0 9.6 %collective-permute-start.27 = (bf16[128,1152]{1,0:T(8,128)(2,1)S(1)}, bf16[128,1152]{1,0:T(8,128)(2,1)S(1)}, u32[]{:S(2)}, u32[]{:S(2)}) collective-permute-start(bf16[128,1152]{1,0:T(8,128)(2,1)S(1)} %get-tuple-element.109), channel_id=1, source_target_pairs={{0,96},{8,104},{16,112},{24,120},{32,0},{40,8},{48,16},{56,24},{64... | collective-permute-start | bytes 884744 | tf_op jit(solution)/shard_map/ppermute | solution.py:275
  187.4 7.5 %collective-permute-start.28 = (bf16[128,1152]{1,0:T(8,128)(2,1)S(1)}, bf16[128,1152]{1,0:T(8,128)(2,1)S(1)}, u32[]{:S(2)}, u32[]{:S(2)}) collective-permute-start(bf16[128,1152]{1,0:T(8,128)(2,1)S(1)} %get-tuple-element.111), channel_id=1, source_target_pairs={{0,128},{8,136},{16,144},{24,152},{32,160},{40,168},{48,176},{56,1... | collective-permute-start | bytes 884744 | tf_op jit(solution)/shard_map/ppermute | solution.py:275
  (21 other events, 52.7 us)
